TPU v7x, 256 devices: a whole 4x4x8 slice. The times are simulated.
256 devices in a mesh: view: 8 (over y, x_lo), tok: 32 (over x_hi, z, core).
Axes of the slice: x: 4 (x_hi: 2, x_lo: 2; x = x_hi * 2 + x_lo), y: 4, z: 8, core: 2. Of those that a mesh axis runs over, the one named last changes fastest.
Arguments:
- queries: bfloat16 [8, 4096, 128], P('view', 'tok'), may hold values from -32 to 32
- keys: bfloat16 [8, 4096, 128], P('view', 'tok'), may hold values from -12 to 12
- values: bfloat16 [8, 4096, 128], P('view', 'tok'), may hold values from -6 to 6
- out_grad: bfloat16 [8, 4096, 128], P('view', 'tok'), may hold values from -24 to 24
- poses: float32 [16, 4, 4], replicated, may hold values from -1 to 1, as said below
- pose_index: int32 [8], replicated, may hold values from 0 to 15
Outputs:
- query_grad: bfloat16 [8, 4096, 128], P('view', 'tok')
- key_grad: bfloat16 [8, 4096, 128], P('view', 'tok')
- value_grad: bfloat16 [8, 4096, 128], P('view', 'tok')
Inputs may be any that keep to these rules, and one draw needn't show every extreme that they name: `poses`: each row of the table is a rigid motion: a rotation in the upper left 3 x 3 block, a translation in the upper right column, and the bottom row 0 0 0 1.
All inputs are finite; a program needn't handle non-finite values.
Results may differ from a plain program's by a relative error of at most 0.022.
The roundings to bfloat16 on the way count: a program that leaves them out, or rounds other values in their place, can miss the bound.
Values may be sent and summed in bfloat16 or wider, within the bound.
A program may use at most 64 MiB of HBM per device.

v0:
```python
import math

import jax
import jax.numpy as jnp
from jax import lax
from jax.sharding import PartitionSpec as P


def combined_all(shard, axis, combine):
    everything = jax.tree.map(lambda part: lax.all_gather(part, axis), shard)
    leading = jax.tree.map(lambda part: part[0], everything)

    def hop(k, so_far):
        return combine(so_far, jax.tree.map(lambda part: part[k], everything))

    return lax.fori_loop(1, lax.axis_size(axis), hop, leading)


def inverse_pose(matrix):
    rotation = matrix[:3, :3].T
    shifted = -jnp.dot(rotation, matrix[:3, 3], precision=lax.Precision.HIGHEST)
    top_rows = jnp.concatenate([rotation, shifted[:, None]], axis=1)
    return jnp.concatenate([top_rows, matrix[3:4, :]], axis=0)


def block_matrix(matrix, feature_dim):
    return jnp.kron(jnp.eye(feature_dim // 4, dtype=jnp.float32), matrix)


def transform(row_block, weight_table):
    return jnp.dot(row_block.astype(jnp.float32), weight_table, precision=lax.Precision.HIGHEST)


def combine(earlier, second):
    row_peak = jnp.maximum(earlier[0], second[0])
    first_factor = jnp.exp(earlier[0] - row_peak)
    second_factor = jnp.exp(second[0] - row_peak)
    return (
        row_peak,
        earlier[1] * first_factor + second[1] * second_factor,
        earlier[2] * first_factor + second[2] * second_factor,
    )


def local_tile(query_all, grad_all, key_all, value_all, merge_rows):
    feature_dim = query_all.shape[1]
    score_scale = feature_dim ** (-0.5)
    row_count = query_all.shape[0]
    block_rows = math.gcd(row_count, 512)
    block_count = row_count // block_rows
    query_blocks = query_all.reshape(block_count, block_rows, feature_dim)
    grad_blocks = grad_all.reshape(block_count, block_rows, feature_dim)

    def statistics(pieces):
        query_block, grad_block = pieces
        scores = (
            jnp.einsum("qd,kd->qk", query_block, key_all, preferred_element_type=jnp.float32)
            * score_scale
        )
        row_peak = jnp.max(scores, axis=1)
        weights = jnp.exp(scores - row_peak[:, None])
        slopes = jnp.einsum("qd,kd->qk", grad_block, value_all, preferred_element_type=jnp.float32)
        return (row_peak, jnp.sum(weights, axis=1), jnp.sum(weights * slopes, axis=1))

    row_peak, row_mass, row_moment = lax.map(statistics, (query_blocks, grad_blocks))
    row_peak, row_mass, row_moment = merge_rows(
        (row_peak.reshape(row_count), row_mass.reshape(row_count), row_moment.reshape(row_count))
    )
    log_mass = (row_peak + jnp.log(row_mass)).reshape(block_count, block_rows)
    centre = (row_moment / row_mass).reshape(block_count, block_rows)

    def accumulate(carry, pieces):
        key_acc, value_acc = carry
        query_block, grad_block, log_block, centre_block = pieces
        scores = (
            jnp.einsum("qd,kd->qk", query_block, key_all, preferred_element_type=jnp.float32)
            * score_scale
        )
        probs = jnp.exp(scores - log_block[:, None])
        slopes = jnp.einsum("qd,kd->qk", grad_block, value_all, preferred_element_type=jnp.float32)
        probs_half = probs.astype(jnp.bfloat16)
        dscores_half = (probs * (slopes - centre_block[:, None])).astype(jnp.bfloat16)
        query_part = (
            jnp.einsum("qk,kd->qd", dscores_half, key_all, preferred_element_type=jnp.float32)
            * score_scale
        )
        key_acc = (
            key_acc
            + jnp.einsum("qk,qd->kd", dscores_half, query_block, preferred_element_type=jnp.float32)
            * score_scale
        )
        value_acc = value_acc + jnp.einsum(
            "qk,qd->kd", probs_half, grad_block, preferred_element_type=jnp.float32
        )
        return ((key_acc, value_acc), query_part)

    empty_grad = jnp.zeros(key_all.shape, jnp.float32)
    (key_acc, value_acc), query_parts = lax.scan(
        accumulate, (empty_grad, empty_grad), (query_blocks, grad_blocks, log_mass, centre)
    )
    return (query_parts.reshape(row_count, feature_dim), key_acc, value_acc)


def per_device(queries, keys, values, out_grad, poses, pose_index):
    feature_dim = queries.shape[2]
    view_id = lax.axis_index("view")
    matrix = poses[pose_index[view_id]]
    forward_table = block_matrix(matrix, feature_dim)
    backward_table = block_matrix(inverse_pose(matrix).T, feature_dim)
    query_turned = transform(queries[0], forward_table).astype(jnp.bfloat16)
    key_turned = transform(keys[0], backward_table).astype(jnp.bfloat16)
    value_turned = transform(values[0], backward_table).astype(jnp.bfloat16)
    grad_turned = transform(out_grad[0], forward_table).astype(jnp.bfloat16)
    query_all, grad_all = (
        lax.all_gather(query_turned, "view", axis=0, tiled=True),
        lax.all_gather(grad_turned, "view", axis=0, tiled=True),
    )
    key_all, value_all = (
        lax.all_gather(key_turned, "tok", axis=0, tiled=True),
        lax.all_gather(value_turned, "tok", axis=0, tiled=True),
    )

    def merge_rows(partial_stats):
        return combined_all(partial_stats, "view", combine)

    query_part, key_part, value_part = local_tile(
        query_all, grad_all, key_all, value_all, merge_rows
    )
    query_sum = lax.psum_scatter(
        query_part.astype(jnp.bfloat16), "view", scatter_dimension=0, tiled=True
    ).astype(jnp.float32)
    key_sum, value_sum = (
        lax.psum_scatter(
            key_part.astype(jnp.bfloat16), "tok", scatter_dimension=0, tiled=True
        ).astype(jnp.float32),
        lax.psum_scatter(
            value_part.astype(jnp.bfloat16), "tok", scatter_dimension=0, tiled=True
        ).astype(jnp.float32),
    )
    query_grad = transform(query_sum, forward_table.T).astype(jnp.bfloat16)[None]
    key_grad = transform(key_sum, backward_table.T).astype(jnp.bfloat16)[None]
    value_grad = transform(value_sum, backward_table.T).astype(jnp.bfloat16)[None]
    return (query_grad, key_grad, value_grad)


def solution(mesh):
    in_specs = (
        P("view", "tok", None),
        P("view", "tok", None),
        P("view", "tok", None),
        P("view", "tok", None),
        P(),
        P(),
    )
    out_specs = (P("view", "tok", None), P("view", "tok", None), P("view", "tok", None))
    return jax.shard_map(
        per_device, mesh=mesh, in_specs=in_specs, out_specs=out_specs, check_vma=False
    )
```

profile of v0, /device:TPU:1, one launch (start us, length us, event | category | flops | bytes accessed | tf_op | source)
XLA Modules:
  0.0 570.0 jit_solution(3981676292290908092)
XLA Ops:
  12.5 1.9 broadcast_multiply_fusion
  14.4 1.6 mul.130
  18.0 3.2 mul.127
  21.5 22.3 %all_gather.21 = bf16[1024,128]{0,1:T(8,128)(2,1)S(1)} all-gather(bf16[128,128]{0,1:T(8,128)(2,1)S(1)} %fusion.29), channel_id=1, replica_groups=mesh['view'=8,'tok'=32] {'view'}, dimensions={0}, use_global_device_ids=true | all-gather | bytes 294912 | tf_op jit(solution)/shard_map/all_gather | solution.py:115
  44.2 20.5 %all_gather.23 = bf16[1024,128]{0,1:T(8,128)(2,1)S(1)} all-gather(bf16[128,128]{0,1:T(8,128)(2,1)S(1)} %fusion.31), channel_id=1, replica_groups=mesh['view'=8,'tok'=32] {'view'}, dimensions={0}, use_global_device_ids=true | all-gather | bytes 294912 | tf_op jit(solution)/shard_map/all_gather | solution.py:116
  65.5 28.2 %all-gather.8.cloned.1.call-done = bf16[4096,128]{0,1:T(8,128)(2,1)} async-done(((bf16[128,128]{0,1:T(8,128)(2,1)}), bf16[4096,128]{0,1:T(8,128)(2,1)}) %all-gather.8.cloned.1.call-update) | async-done | bytes 1048592 | tf_op jit(solution)/shard_map/all_gather | solution.py:120
  93.7 2.3 copy.31
  96.0 70.5 %all-gather.6.cloned.1.call-done = bf16[4096,128]{0,1:T(8,128)(2,1)} async-done(((bf16[128,128]{0,1:T(8,128)(2,1)}), bf16[4096,128]{0,1:T(8,128)(2,1)}) %all-gather.6.cloned.1.call-update) | async-done | bytes 1048592 | tf_op jit(solution)/shard_map/all_gather | solution.py:119
  166.5 1.6 copy.33
  168.1 10.9 %while.48 = (s32[]{:T(128)}, f32[2,512]{1,0:T(2,128)S(1)}, f32[2,512]{1,0:T(2,128)S(1)}, f32[2,512]{1,0:T(2,128)S(1)}, bf16[2,512,128]{2,1,0:T(8,128)(2,1)S(1)},...) while((s32[]{:T(128)}, f32[2,512]{1,0:T(2,128)S(1)}, ...), condition=%wide.region_4.5_spmd, body=%wide.region_0.4_spmd.sunk | while | flops 1092614656 | bytes 32790712 | solution.py:65
  169.5 2.4 multiply_reduce_fusion.5
  172.0 1.5 fusion.82
  175.0 2.4 multiply_reduce_fusion.5
  177.4 1.5 fusion.82
  179.1 21.8 %all-gather.1 = f32[8,1,1024]{2,1,0:T(1,128)S(1)} all-gather(f32[1,1,1024]{2,1,0:T(1,128)S(1)} %reshape.80), channel_id=1, replica_groups=mesh['view'=8,'tok'=32] {'view'}, dimensions={0}, use_global_device_ids=true | all-gather | bytes 36864 | tf_op jit(solution)/shard_map/all_gather | solution.py:10
  201.5 21.7 %all-gather = f32[8,1,1024]{2,1,0:T(1,128)S(1)} all-gather(f32[1,1,1024]{2,1,0:T(1,128)S(1)} %reshape.78), channel_id=1, replica_groups=mesh['view'=8,'tok'=32] {'view'}, dimensions={0}, use_global_device_ids=true | all-gather | bytes 36864 | tf_op jit(solution)/shard_map/all_gather | solution.py:10
  223.3 21.9 %all-gather.2 = f32[8,1,1024]{2,1,0:T(1,128)S(1)} all-gather(f32[1,1,1024]{2,1,0:T(1,128)S(1)} %reshape.82), channel_id=1, replica_groups=mesh['view'=8,'tok'=32] {'view'}, dimensions={0}, use_global_device_ids=true | all-gather | bytes 36864 | tf_op jit(solution)/shard_map/all_gather | solution.py:10
  245.8 6.1 %while.49 = (s32[]{:T(128)}, f32[1024]{0:T(1024)S(1)}, f32[1024]{0:T(1024)S(1)}, f32[1024]{0:T(1024)S(1)}, f32[8,1024]{1,0:T(8,128)S(1)}, /*index=5*/f32[8,1024]...) while((s32[]{:T(128)}, f32[1024]{0:T(1024)S(1)}, f32[1024]{0:T(1024)S(1)}, ...), condition=%wide.region_6.7_spmd, body=%wide.region_5.6_spmd.sunk | while | flops 11269 | bytes 82063 | solution.py:16
  252.0 23.3 %while.50 = (s32[]{:T(128)}, f32[4096,128]{1,0:T(8,128)}, f32[4096,128]{1,0:T(8,128)S(1)}, bf16[2,512,128]{2,1,0:T(8,128)(2,1)}, bf16[2,512,128]{2,1,0:T(8,128)(...) while((s32[]{:T(128)}, f32[4096,128]{1,0:T(8,128)}, ...), condition=%wide.region_8.9_spmd.clone, body=%wide.region_7.8_spmd.clone.sunk | while | flops 2703818752 | bytes 74201408 | solution.py:98
  253.3 2.6 convolution_add_fusion.2
  255.9 2.6 multiply_convert_fusion.2
  260.1 2.1 fusion.94
  264.9 2.6 convolution_add_fusion.2
  267.6 2.6 multiply_convert_fusion.2
  271.8 2.1 fusion.94
  275.3 2.7 convert_element_type.80
  279.2 47.1 %reduce-scatter.4.cloned.1.call-done = bf16[128,128]{1,0:T(8,128)(2,1)} async-done(((bf16[1024,128]{1,0:T(8,128)(2,1)}), bf16[128,128]{1,0:T(8,128)(2,1)}) %reduce-scatter.4.cloned.1.call-update) | async-done | bytes 32784 | tf_op jit(solution)/shard_map/reduce_scatter | solution.py:129
  326.3 1.6 fusion.33
  327.9 116.6 %reduce-scatter.6.cloned.1.call-done = bf16[128,128]{1,0:T(8,128)(2,1)} async-done(((bf16[4096,128]{1,0:T(8,128)(2,1)}), bf16[128,128]{1,0:T(8,128)(2,1)}) %reduce-scatter.6.cloned.1.call-update) | async-done | bytes 32784 | tf_op jit(solution)/shard_map/reduce_scatter | solution.py:133
  444.5 1.6 fusion.34
  446.1 115.7 %reduce-scatter.8.cloned.1.call-done = bf16[128,128]{1,0:T(8,128)(2,1)} async-done(((bf16[4096,128]{1,0:T(8,128)(2,1)}), bf16[128,128]{1,0:T(8,128)(2,1)}) %reduce-scatter.8.cloned.1.call-update) | async-done | bytes 32784 | tf_op jit(solution)/shard_map/reduce_scatter | solution.py:136
  561.9 1.6 fusion.35
  (136 shorter events, 26.3 us)
Async XLA Ops:
  7.2 8.9 %copy-start = (bf16[1,128,128]{2,1,0:T(8,128)(2,1)S(1)}, bf16[1,128,128]{2,1,0:T(8,128)(2,1)}, u32[]{:S(2)}) copy-start(bf16[1,128,128]{2,1,0:T(8,128)(2,1)} %param.14) | copy-start | bytes 98308
  7.2 9.8 %copy-start.11 = (bf16[1,128,128]{2,1,0:T(8,128)(2,1)S(1)}, bf16[1,128,128]{2,1,0:T(8,128)(2,1)}, u32[]{:S(2)}) copy-start(bf16[1,128,128]{2,1,0:T(8,128)(2,1)} %param.13) | copy-start | bytes 98308
  7.2 86.5 %all-gather.8.cloned.1.call-start = ((), (), s32[]{:S(2)}) async-start(), calls=%async_computation.4 | async-start | bytes 1081344 | tf_op jit(solution)/shard_map/all_gather | solution.py:120
  12.5 8.7 %copy-start.12 = (bf16[1,128,128]{2,1,0:T(8,128)(2,1)S(1)}, bf16[1,128,128]{2,1,0:T(8,128)(2,1)}, u32[]{:S(2)}) copy-start(bf16[1,128,128]{2,1,0:T(8,128)(2,1)} %param.12) | copy-start | bytes 98308
  12.5 31.5 %copy-start.13 = (bf16[1,128,128]{2,1,0:T(8,128)(2,1)S(1)}, bf16[1,128,128]{2,1,0:T(8,128)(2,1)}, u32[]{:S(2)}) copy-start(bf16[1,128,128]{2,1,0:T(8,128)(2,1)} %param.15) | copy-start | bytes 98308
  16.9 149.6 %all-gather.6.cloned.1.call-start = ((), (), s32[]{:S(2)}) async-start(), calls=%async_computation.3 | async-start | bytes 1081344 | tf_op jit(solution)/shard_map/all_gather | solution.py:119
  17.9 308.4 %reduce-scatter.4.cloned.1.call-start = ((), (), s32[]{:S(2)}) async-start(), calls=%async_computation.5 | async-start | bytes 294912 | tf_op jit(solution)/shard_map/reduce_scatter | solution.py:129
  21.2 74.8 %copy-start.7 = (f32[128,128]{1,0:T(8,128)}, f32[128,128]{1,0:T(8,128)S(1)}, u32[]{:S(2)}) copy-start(f32[128,128]{1,0:T(8,128)S(1)} %mul.127) | copy-start | bytes 196612
  168.2 1.4 copy-start.3
  168.2 1.4 copy-start.5
  173.6 1.4 copy-start.3
  173.6 1.4 copy-start.5
  252.0 1.3 copy-start.6
  253.3 2.6 copy-start.4
  255.9 2.6 copy-start.9
  258.5 1.6 copy-start.1
  260.1 2.1 copy-start.10
  262.3 1.3 copy-start.2
  263.6 1.3 copy-start.6
  264.9 2.6 copy-start.4
  267.5 2.6 copy-start.9
  270.2 1.6 copy-start.1
  271.8 2.1 copy-start.10
  273.9 1.3 copy-start.2
  275.3 169.3 %reduce-scatter.6.cloned.1.call-start = ((), (), s32[]{:S(2)}) async-start(), calls=%async_computation.6 | async-start | bytes 1081344 | tf_op jit(solution)/shard_map/reduce_scatter | solution.py:133
  275.3 51.0 %copy-start.8 = (f32[128,128]{1,0:T(8,128)S(1)}, f32[128,128]{1,0:T(8,128)}, u32[]{:S(2)}) copy-start(f32[128,128]{1,0:T(8,128)} %copy-done.7) | copy-start | bytes 196612
  278.1 283.8 %reduce-scatter.8.cloned.1.call-start = ((), (), s32[]{:S(2)}) async-start(), calls=%async_computation.7 | async-start | bytes 1081344 | tf_op jit(solution)/shard_map/reduce_scatter | solution.py:136
Sparse Core Ops, SparseCore 0:
  17.0 76.6 all-gather.7
  96.8 69.6 all-gather.5
  275.4 50.8 reduce-scatter.3
  330.8 113.6 reduce-scatter.5
  448.5 113.3 reduce-scatter.7
where the time goes:
time: 575 us; the launch traced here: 570 us
  waiting for transfers between devices  378 us (66%)
  blocking collectives  108 us (19%)
  matrix products  34.5 us (6%)
  local copies, waits for them, and re-layouts  23.3 us (4%)
  between operations  15.9 us (3%)
  other arithmetic  8.98 us (2%)
    reduce_scatter x1, waiting for transfers between devices, per_device(): lax.psum_scatter(key_part.astype(jnp.bfloat16), 'tok', scatter_dimension=...  117 us
    reduce_scatter x1, waiting for transfers between devices, per_device(): lax.psum_scatter(value_part.astype(jnp.bfloat16), 'tok', scatter_dimensio...  116 us
    all_gather x1, waiting for transfers between devices, per_device(): lax.all_gather(key_turned, 'tok', axis=0, tiled=True)  70.5 us
    all_gather x3, blocking collectives, combined_all(): everything = jax.tree.map(lambda part: lax.all_gather(part, axis), shard)  65.4 us
    reduce_scatter x1, waiting for transfers between devices, per_device(): lax.psum_scatter(query_part.astype(jnp.bfloat16), 'view', scatter_dimensi...  47.1 us
    all_gather x1, waiting for transfers between devices, per_device(): lax.all_gather(value_turned, 'tok', axis=0, tiled=True)  28.2 us
    all_gather x1, blocking collectives, per_device(): lax.all_gather(query_turned, 'view', axis=0, tiled=True)  22.3 us
    all_gather x1, blocking collectives, per_device(): lax.all_gather(grad_turned, 'view', axis=0, tiled=True)  20.5 us
  transfers between devices with their start and end apart: 5, of which 5 were waited for; matrix products, arithmetic and copies ran while one was open for 3% of the time, Pallas kernels for 0%

commit v1 on v0

v1 whole, which is shorter than its diff:
```python
import math

import jax
import jax.numpy as jnp
from jax import lax
from jax.experimental import pallas as pl
from jax.experimental.pallas import tpu as pltpu
from jax.sharding import PartitionSpec as P

F32 = jnp.float32
BF16 = jnp.bfloat16
MESH = pl.DeviceIdType.MESH
HD = 128
TOK = 128
XS, YS, ZS = 4, 4, 8
ROWS = XS * YS * TOK
COLS = ZS * 2 * TOK
SCALE = HD**-0.5
SCALE2 = SCALE / math.log(2.0)
SEMS = 56


def nt(a, b):
    return lax.dot_general(a, b, (((1,), (1,)), ((), ())), preferred_element_type=F32)


def nn(a, b):
    return lax.dot_general(a, b, (((1,), (0,)), ((), ())), preferred_element_type=F32)


def turned(a, b, b_dim):
    return lax.dot_general(
        a, b, (((1,), (b_dim,)), ((), ())),
        precision=lax.Precision.HIGHEST, preferred_element_type=F32,
    )


def tables(poses, pose_index, view):
    row = pose_index[view]
    mat = [[poses[row, i, j] for j in range(4)] for i in range(4)]
    back = [[mat[i][j] for j in range(3)] + [mat[3][i]] for i in range(3)]
    back.append(
        [-(mat[0][j] * mat[0][3] + mat[1][j] * mat[1][3] + mat[2][j] * mat[2][3]) for j in range(3)]
        + [mat[3][3]]
    )
    i = lax.broadcasted_iota(jnp.int32, (HD, HD), 0)
    j = lax.broadcasted_iota(jnp.int32, (HD, HD), 1)
    place = jnp.where(i // 4 == j // 4, (i % 4) * 4 + j % 4, 16)
    forward = jnp.zeros((HD, HD), F32)
    backward = jnp.zeros((HD, HD), F32)
    for a in range(4):
        for b in range(4):
            here = place == 4 * a + b
            forward = jnp.where(here, mat[a][b], forward)
            backward = jnp.where(here, back[a][b], backward)
    return forward, backward


def kernel(
    q_ref, k_ref, v_ref, g_ref, poses, pose_index, dq_ref, dk_ref, dv_ref,
    qb, gb, kv, sc, sl, st, stx, sty, dkf, dvf, dqt,
    pair_out, pair_in, ring_out, ring_in, qa, qa_in, qa_mid, qa_fin, qc, qc_in, qc_mid, qc_fin,
    fwd, bwd, send_sem, recv_sem,
):
    view = lax.axis_index("view")
    tok = lax.axis_index("tok")
    y = view // 2
    x = (tok // 16) * 2 + view % 2
    z = (tok // 2) % 8
    c = tok % 2
    taken = [0]
    pending = []

    def device(dx=0, dy=0, dz=0, dc=0):
        px, py, pz, pc = (x + dx) % XS, (y + dy) % YS, (z + dz) % ZS, (c + dc) % 2
        return (py * 2 + px % 2, ((px // 2) * ZS + pz) * 2 + pc)

    def copy(src, dst, to, arrives):
        n = taken[0]
        taken[0] += 1
        out = pltpu.make_async_remote_copy(
            src_ref=src, dst_ref=dst, send_sem=send_sem.at[n], recv_sem=recv_sem.at[n],
            device_id=to, device_id_type=MESH,
        )
        out.start()
        pending.append((src, send_sem.at[n]))
        return lambda: pltpu.make_async_copy(arrives, arrives, recv_sem.at[n]).wait()

    barrier = pltpu.get_barrier_semaphore()
    peers = [dict(dx=d) for d in (1, 2, 3)] + [dict(dy=d) for d in (1, 2, 3)]
    peers += [dict(dz=1), dict(dz=ZS - 1), dict(dc=1)]
    for peer in peers:
        pl.semaphore_signal(barrier, inc=1, device_id=device(**peer), device_id_type=MESH)

    forward, backward = tables(poses, pose_index, view)
    fwd[...] = forward
    bwd[...] = backward
    qb[y, x] = turned(q_ref[0].astype(F32), forward, 0).astype(BF16)
    gb[x, y] = turned(g_ref[0].astype(F32), forward, 0).astype(BF16)
    kv[z, c, 0] = turned(k_ref[0].astype(F32), backward, 0).astype(BF16)
    kv[z, c, 1] = turned(v_ref[0].astype(F32), backward, 0).astype(BF16)
    pl.semaphore_wait(barrier, len(peers))

    def zat(d):
        return (z + d + ZS) % ZS

    q_first = [copy(qb.at[y, x], qb.at[y, x], device(dx=d), qb.at[y, (x + XS - d) % XS]) for d in (1, 3, 2)]
    g_first = [copy(gb.at[x, y], gb.at[x, y], device(dy=d), gb.at[x, (y + YS - d) % YS]) for d in (1, 3, 2)]
    shared = [copy(kv.at[z, c], kv.at[z, c], device(dc=1), kv.at[z, 1 - c])]
    half = (slice(None), slice(None))

    def ring(t):
        if t < ZS // 2:
            right = copy(kv.at[zat(1 - t), c], kv.at[zat(1 - t), c], device(dz=1), kv.at[zat(-t), c])
            left = copy(kv.at[zat(t - 1), c], kv.at[zat(t - 1), c], device(dz=ZS - 1), kv.at[zat(t), c])
        else:
            right = copy(kv.at[zat(1 - t), c, 0], kv.at[zat(1 - t), c, 0], device(dz=1), kv.at[zat(-t), c, 0])
            left = copy(kv.at[zat(t - 1), c, 1], kv.at[zat(t - 1), c, 1], device(dz=ZS - 1), kv.at[zat(t), c, 1])
        return right, left

    def share(t):
        if t < ZS // 2:
            for w in (zat(-t), zat(t)):
                shared.append(copy(kv.at[w, c], kv.at[w, c], device(dc=1), kv.at[w, 1 - c]))
        else:
            for part, w in ((0, zat(-t)), (1, zat(t))):
                shared.append(copy(kv.at[w, c, part], kv.at[w, c, part], device(dc=1), kv.at[w, 1 - c, part]))

    arriving = ring(1)
    for t in range(1, ZS // 2 + 1):
        for wait in arriving:
            wait()
        if t < ZS // 2:
            arriving = ring(t + 1)
        share(t)
        if t == 1:
            for wait in q_first:
                wait()
            q_second = [copy(qb.at[y], qb.at[y], device(dy=d), qb.at[(y + YS - d) % YS]) for d in (1, 3, 2)]
            for wait in g_first:
                wait()
            g_second = [copy(gb.at[x], gb.at[x], device(dx=d), gb.at[(x + XS - d) % XS]) for d in (1, 3, 2)]
    for wait in shared + q_second + g_second:
        wait()

    keys = kv[:, :, 0].reshape(COLS, HD)
    vals = kv[:, :, 1].reshape(COLS, HD)

    def statistics(r, carry):
        ry, rx = r // XS, r % XS
        cols = pl.ds(pl.multiple_of(r * TOK, TOK), TOK)
        s = nt(kv[:, :, 0].reshape(COLS, HD), qb[ry, rx]) * SCALE2
        p = nt(kv[:, :, 1].reshape(COLS, HD), gb[rx, ry])
        sc[:, cols] = s
        sl[:, cols] = p
        s = s.reshape(COLS // 8, 8, TOK)
        peak = jnp.max(s, axis=0)
        w = jnp.exp2(s - peak[None])
        mass = jnp.sum(w, axis=0)
        moment = jnp.sum(w * p.reshape(COLS // 8, 8, TOK), axis=0)
        top = jnp.max(peak, axis=0, keepdims=True)
        factor = jnp.exp2(peak - top)
        mass = jnp.sum(mass * factor, axis=0, keepdims=True)
        moment = jnp.sum(moment * factor, axis=0, keepdims=True)
        st[0, pl.ds(r, 1), :] = top + jnp.log2(mass)
        st[1, pl.ds(r, 1), :] = moment / mass
        return carry

    lax.fori_loop(0, XS * YS, statistics, 0)

    def merge(parts):
        logs = [part[0] for part in parts]
        top = logs[0]
        for log in logs[1:]:
            top = jnp.maximum(top, log)
        weights = [jnp.exp2(log - top) for log in logs]
        mass = weights[0]
        moment = weights[0] * parts[0][1]
        for weight, part in zip(weights[1:], parts[1:]):
            mass = mass + weight
            moment = moment + weight * part[1]
        return top + jnp.log2(mass), moment / mass

    def exchange(source, landing, axis):
        waits = [copy(source, landing.at[d - 1], device(**{axis: d}), landing.at[d - 1]) for d in (1, 3, 2)]
        for wait in waits:
            wait()

    exchange(st, stx, "dx")
    log_mass, centre = merge([st] + [stx.at[d] for d in range(3)])
    sty[3, 0] = log_mass
    sty[3, 1] = centre
    exchange(sty.at[3], sty, "dy")
    log_mass, centre = merge([sty.at[3]] + [sty.at[d] for d in range(3)])
    st2 = stx.at[0]
    st2[0] = log_mass
    st2[1] = centre

    dqt[...] = jnp.zeros_like(dqt)

    def gradients(i, carry):
        cols = pl.ds(pl.multiple_of(i * 512, 512), 512)
        zs = pl.ds(i * 2, 2)
        kt = kv[zs, :, 0].reshape(512, HD).T
        dk = jnp.zeros((512, HD), F32)
        dv = jnp.zeros((512, HD), F32)
        for ry in range(YS):
            rows = slice(ry * 512, ry * 512 + 512)
            log_row = jnp.concatenate([st2[0, ry * 4 + n : ry * 4 + n + 1, :] for n in range(4)], axis=1)
            centre_row = jnp.concatenate([st2[1, ry * 4 + n : ry * 4 + n + 1, :] for n in range(4)], axis=1)
            probs = jnp.exp2(sc[cols, rows] - log_row)
            ds = (probs * (sl[cols, rows] - centre_row)).astype(BF16)
            dk = dk + nn(ds, qb[ry].reshape(512, HD))
            dv = dv + nn(probs.astype(BF16), gb[:, ry].reshape(512, HD))
            dqt[:, rows] += nn(kt, ds)
        dkf[zs] = dk.reshape(2, 2, TOK, HD)
        dvf[zs] = dv.reshape(2, 2, TOK, HD)
        return carry

    lax.fori_loop(0, COLS // 512, gradients, 0)

    for w in range(ZS):
        pair_out[w, 0] = dkf[w, 1 - c].astype(BF16)
        pair_out[w, 1] = dvf[w, 1 - c].astype(BF16)
    pair = copy(pair_out, pair_in, device(dc=1), pair_in)
    for ry in range(YS):
        for rx in range(XS):
            r = ry * XS + rx
            block = dqt[:, r * TOK : r * TOK + TOK].astype(BF16)
            qa[ry, rx] = block[: HD // 2]
            qc[rx, ry] = block[HD // 2 :]
    a_waits = [copy(qa.at[(y + d) % YS], qa_in.at[d - 1], device(dy=d), qa_in.at[d - 1]) for d in (1, 3, 2)]
    c_waits = [copy(qc.at[(x + d) % XS], qc_in.at[d - 1], device(dx=d), qc_in.at[d - 1]) for d in (1, 3, 2)]
    pair()

    def own(w, part):
        return (dkf, dvf)[part][w, c] + pair_in[w, part].astype(F32)

    last = ZS // 2
    for t in range(1, last + 1):
        far = last + 1 - t
        right_parts = (0,) if t == 1 else (0, 1)
        left_parts = (1,) if t == 1 else (0, 1)
        for way, w, parts in ((0, zat(far), right_parts), (1, zat(-far), left_parts)):
            for part in parts:
                total = own(w, part)
                if t > 2 or (t == 2 and part == way):
                    total = total + ring_in[way, t - 2, part].astype(F32)
                ring_out[way, t - 1, part] = total.astype(BF16)
        if t == 1:
            waits = [
                copy(ring_out.at[w, 0, w], ring_in.at[w, 0, w], device(dz=(1, ZS - 1)[w]), ring_in.at[w, 0, w])
                for w in (0, 1)
            ]
        else:
            waits = [
                copy(ring_out.at[w, t - 1], ring_in.at[w, t - 1], device(dz=(1, ZS - 1)[w]), ring_in.at[w, t - 1])
                for w in (0, 1)
            ]
        if t == 1:
            for wait in a_waits:
                wait()
            qa_mid[...] = (
                qa[y].astype(F32) + qa_in[0].astype(F32) + qa_in[1].astype(F32) + qa_in[2].astype(F32)
            ).astype(BF16)
            a_waits = [copy(qa_mid.at[(x + d) % XS], qa_fin.at[d - 1], device(dx=d), qa_fin.at[d - 1]) for d in (1, 3, 2)]
            for wait in c_waits:
                wait()
            qc_mid[...] = (
                qc[x].astype(F32) + qc_in[0].astype(F32) + qc_in[1].astype(F32) + qc_in[2].astype(F32)
            ).astype(BF16)
            c_waits = [copy(qc_mid.at[(y + d) % YS], qc_fin.at[d - 1], device(dy=d), qc_fin.at[d - 1]) for d in (1, 3, 2)]
        for wait in waits:
            wait()
    for wait in a_waits + c_waits:
        wait()
    dk = own(z, 0) + ring_in[0, last - 1, 0].astype(F32) + ring_in[1, last - 1, 0].astype(F32)
    dv = own(z, 1) + ring_in[0, last - 1, 1].astype(F32) + ring_in[1, last - 1, 1].astype(F32)
    top = qa_mid[x].astype(F32) + qa_fin[0].astype(F32) + qa_fin[1].astype(F32) + qa_fin[2].astype(F32)
    low = qc_mid[y].astype(F32) + qc_fin[0].astype(F32) + qc_fin[1].astype(F32) + qc_fin[2].astype(F32)
    dq = jnp.concatenate([top, low], axis=0).T
    dq_ref[0] = (turned(dq, fwd[...], 1) * SCALE).astype(BF16)
    dk_ref[0] = (turned(dk, bwd[...], 1) * SCALE).astype(BF16)
    dv_ref[0] = turned(dv, bwd[...], 1).astype(BF16)
    for src, sem in pending:
        pltpu.make_async_copy(src, src, sem).wait()
    assert taken[0] <= SEMS


def per_device(queries, keys, values, out_grad, poses, pose_index):
    block = jax.ShapeDtypeStruct((1, TOK, HD), BF16)
    vmem = pl.BlockSpec(memory_space=pltpu.VMEM)
    smem = pl.BlockSpec(memory_space=pltpu.SMEM)

    def buf(*shape, kind=BF16):
        return pltpu.VMEM(shape, kind)

    half = HD // 2
    return pl.pallas_call(
        kernel,
        out_shape=(block, block, block),
        in_specs=[vmem] * 4 + [smem] * 2,
        out_specs=(vmem, vmem, vmem),
        scratch_shapes=[
            buf(YS, XS, TOK, HD), buf(XS, YS, TOK, HD), buf(ZS, 2, 2, TOK, HD),
            buf(COLS, ROWS, kind=F32), buf(COLS, ROWS, kind=F32),
            buf(2, 16, TOK, kind=F32), buf(3, 2, 16, TOK, kind=F32), buf(4, 2, 16, TOK, kind=F32),
            buf(ZS, 2, TOK, HD, kind=F32), buf(ZS, 2, TOK, HD, kind=F32), buf(HD, ROWS, kind=F32),
            buf(ZS, 2, TOK, HD), buf(ZS, 2, TOK, HD),
            buf(2, 4, 2, TOK, HD), buf(2, 4, 2, TOK, HD),
            buf(YS, XS, half, TOK), buf(3, XS, half, TOK), buf(XS, half, TOK), buf(3, half, TOK),
            buf(XS, YS, half, TOK), buf(3, YS, half, TOK), buf(YS, half, TOK), buf(3, half, TOK),
            buf(HD, HD, kind=F32), buf(HD, HD, kind=F32),
            pltpu.SemaphoreType.DMA((SEMS,)), pltpu.SemaphoreType.DMA((SEMS,)),
        ],
        compiler_params=pltpu.CompilerParams(
            collective_id=0, has_side_effects=True, vmem_limit_bytes=58 * 2**20
        ),
    )(queries, keys, values, out_grad, poses, pose_index)


def solution(mesh):
    block = P("view", "tok", None)
    return jax.shard_map(
        per_device, mesh=mesh, in_specs=(block,) * 4 + (P(), P()), out_specs=(block,) * 3, check_vma=False
    )
```

time: 575 us -> 78.3 us (0.14)
  the two profiles are of different devices: /device:TPU:1 before, /device:TPU:2 now
where the time goes in v1:
time: 78.3 us; the launch traced here: 77.9 us
  Pallas kernels  73.1 us (93%)
  local copies, waits for them, and re-layouts  4.17 us (5%)
    pallas_call x1, Pallas kernels, per_device(): pl.pallas_call(kernel, out_shape=(block, block, block), in_specs=[vmem] *...  73.1 us
    unnamed x8, local copies, waits for them, and re-layouts  4.17 us

profile of v1, /device:TPU:2, one launch (start us, length us, event | category | flops | bytes accessed | tf_op | source)
XLA Modules:
  0.0 77.9 jit_solution(14281938746039409258)
XLA Ops:
  0.6 1.4 %copy.9.poses = f32[16,4,4]{2,1,0:T(4,128)} copy(f32[16,4,4]{0,2,1:T(4,128)} %param.10) | data formatting | bytes 2048 | tf_op args[4]
  2.0 73.1 %shard_map.85 = (bf16[1,128,128]{2,1,0:T(8,128)(2,1)}, bf16[1,128,128]{2,1,0:T(8,128)(2,1)}, bf16[1,128,128]{2,1,0:T(8,128)(2,1)}) custom-call(bf16[1,128,128]{2,1,0:T(8,128)(2,1)} %q_ref.1, bf16[1,128,128]{2,1,0:T(8,128)(2,1)} %k_ref.1, bf16[1,128,128]{2,1,0:T(8,128)(2,1)} %v_ref.1, bf16[1,128,128]{2,1,0:T(8,128)(2,1)} %g_ref.1, f32[16,4,4]{2,1,0:T(4,128)} %copy.9.poses, ...), custom_call_target="tpu_custom_call" | custom-call | tf_op jit(solution)/shard_map/pallas_call | solution.py:299
  75.1 0.0 copy-start.1
  75.1 1.4 %copy.13 = bf16[1,128,128]{2,1,0:T(8,128)(2,1)} copy(bf16[1,128,128]{2,1,0:T(8,128)(2,1)} %get-tuple-element.6) | data formatting | bytes 65536
  76.5 0.0 copy-done.1
  76.5 0.0 copy-start
  76.5 0.6 copy.14
  77.2 0.2 copy-done
  77.3 0.6 copy.15
Async XLA Ops:
  75.1 1.4 %copy-start.1 = (bf16[1,128,128]{2,1,0:T(8,128)(2,1)S(1)}, bf16[1,128,128]{2,1,0:T(8,128)(2,1)}, u32[]{:S(2)}) copy-start(bf16[1,128,128]{2,1,0:T(8,128)(2,1)} %get-tuple-element.7) | copy-start | bytes 98308
  76.5 0.8 copy-start

commit v2 on v1

v2 whole, which is shorter than its diff:
```python
import math

import jax
import jax.numpy as jnp
from jax import lax
from jax.experimental import pallas as pl
from jax.experimental.pallas import tpu as pltpu
from jax.sharding import PartitionSpec as P

F32 = jnp.float32
BF16 = jnp.bfloat16
MESH = pl.DeviceIdType.MESH
HD = 128
TOK = 128
XS, YS, ZS = 4, 4, 8
ROWS = XS * YS * TOK
COLS = ZS * 2 * TOK
SCALE = HD**-0.5
SCALE2 = SCALE / math.log(2.0)
SEMS = 128
HALF = TOK // 2
LANES = ROWS // 2
DIST = (0, 1, -1, 2, -2, 3, -3, 4)
POS = {d: p for p, d in enumerate(DIST)}
UNROLL = 1
NEAR = 5


def nt(a, b):
    return lax.dot_general(a, b, (((1,), (1,)), ((), ())), preferred_element_type=F32)


def nn(a, b):
    return lax.dot_general(a, b, (((1,), (0,)), ((), ())), preferred_element_type=F32)


def turned(a, b, b_dim):
    return lax.dot_general(
        a, b, (((1,), (b_dim,)), ((), ())),
        precision=lax.Precision.HIGHEST, preferred_element_type=F32,
    )


def tables(poses, pose_index, view):
    row = pose_index[view]
    mat = [[poses[i, j, row] for j in range(4)] for i in range(4)]
    back = [[mat[i][j] for j in range(3)] + [mat[3][i]] for i in range(3)]
    back.append(
        [-(mat[0][j] * mat[0][3] + mat[1][j] * mat[1][3] + mat[2][j] * mat[2][3]) for j in range(3)]
        + [mat[3][3]]
    )
    i = lax.broadcasted_iota(jnp.int32, (HD, HD), 0)
    j = lax.broadcasted_iota(jnp.int32, (HD, HD), 1)
    place = jnp.where(i // 4 == j // 4, (i % 4) * 4 + j % 4, 16)
    forward = jnp.zeros((HD, HD), F32)
    backward = jnp.zeros((HD, HD), F32)
    for a in range(4):
        for b in range(4):
            here = place == 4 * a + b
            forward = jnp.where(here, mat[a][b], forward)
            backward = jnp.where(here, back[a][b], backward)
    return forward, backward


def kernel(
    q_ref, k_ref, v_ref, g_ref, poses, pose_index, dq_ref, dk_ref, dv_ref,
    qb, gb, kv, wt, sl, pk, ms, mo, st, stx, mid, sty, fs, cs, dkf, dvf, dqt,
    pair_out, pair_in, red_out, relay_out, red_in,
    qa, qa_in, qa_mid, qa_fin, qc, qc_in, qc_mid, qc_fin, fwd, bwd, send_sem, recv_sem,
):
    view = lax.axis_index("view")
    tok = lax.axis_index("tok")
    y = view // 2
    x = (tok // 16) * 2 + view % 2
    z = (tok // 2) % 8
    c = tok % 2
    taken = [0]
    pending = []

    def device(dx=0, dy=0, dz=0, dc=0):
        px, py, pz, pc = (x + dx) % XS, (y + dy) % YS, (z + dz + ZS) % ZS, (c + dc) % 2
        return (py * 2 + px % 2, ((px // 2) * ZS + pz) * 2 + pc)

    def copy(src, dst, to, arrives=None):
        n = taken[0]
        taken[0] += 1
        arrives = dst if arrives is None else arrives
        pltpu.make_async_remote_copy(
            src_ref=src, dst_ref=dst, send_sem=send_sem.at[n], recv_sem=recv_sem.at[n],
            device_id=device(**to), device_id_type=MESH,
        ).start()
        pending.append((src, send_sem.at[n]))
        return lambda: pltpu.make_async_copy(arrives, arrives, recv_sem.at[n]).wait()

    def done(waits):
        for wait in waits:
            wait()

    barrier = pltpu.get_barrier_semaphore()
    peers = [dict(dx=d) for d in (1, 2, 3)] + [dict(dy=d) for d in (1, 2, 3)]
    peers += [dict(dz=d) for d in (1, -1, 2, -2)] + [dict(dc=1)]
    for peer in peers:
        pl.semaphore_signal(barrier, inc=1, device_id=device(**peer), device_id_type=MESH)

    forward, backward = tables(poses, pose_index, view)
    fwd[...] = forward
    bwd[...] = backward
    kv[0, 0, 0] = turned(k_ref[0].astype(F32), backward, 0).astype(BF16)
    kv[0, 0, 1] = turned(v_ref[0].astype(F32), backward, 0).astype(BF16)
    q_own = turned(q_ref[0].astype(F32), forward, 0).astype(BF16)
    g_own = turned(g_ref[0].astype(F32), forward, 0).astype(BF16)
    for h in range(2):
        qb[h, y, x] = q_own[h * HALF : h * HALF + HALF]
        gb[h, x, y] = g_own[h * HALF : h * HALF + HALF]
    dqt[...] = jnp.zeros_like(dqt)
    pl.semaphore_wait(barrier, len(peers))

    ahead, behind = [None, None], [None, None]
    ahead[0] = copy(kv.at[0, 0, 0], kv.at[POS[-2], 0, 0], dict(dz=2))
    behind[1] = copy(kv.at[0, 0, 1], kv.at[POS[2], 0, 1], dict(dz=-2))
    q_first, g_first, q_second, g_second = [], [], [], []
    for h in range(2):
        q_first.append([
            copy(qb.at[h, y, x], qb.at[h, y, x], dict(dx=d), qb.at[h, y, (x + XS - d) % XS]) for d in (1, 3, 2)
        ])
        g_first.append([
            copy(gb.at[h, x, y], gb.at[h, x, y], dict(dy=d), gb.at[h, x, (y + YS - d) % YS]) for d in (1, 3, 2)
        ])
        if h == 0:
            ahead[1] = copy(kv.at[0, 0, 1], kv.at[POS[-2], 0, 1], dict(dz=2))
            behind[0] = copy(kv.at[0, 0, 0], kv.at[POS[2], 0, 0], dict(dz=-2))
    shared = [copy(kv.at[0, 0], kv.at[0, 1], dict(dc=1))]
    beside = [copy(kv.at[0, 0], kv.at[POS[-1], 0], dict(dz=1)), copy(kv.at[0, 0], kv.at[POS[1], 0], dict(dz=-1))]

    def share(p, part):
        return copy(kv.at[p, 0, part], kv.at[p, 1, part], dict(dc=1))

    for h in range(2):
        done(q_first[h])
        q_second.append([
            copy(qb.at[h, y], qb.at[h, y], dict(dy=d), qb.at[h, (y + YS - d) % YS]) for d in (1, 3, 2)
        ])
        done(g_first[h])
        g_second.append([
            copy(gb.at[h, x], gb.at[h, x], dict(dx=d), gb.at[h, (x + XS - d) % XS]) for d in (1, 3, 2)
        ])
        if h == 0:
            far = {}
            for part, way in ((0, 1), (1, -1)):
                (ahead, behind)[part][part]()
                p = POS[-2 * way]
                far[4, part] = copy(kv.at[p, 0, part], kv.at[POS[4], 0, part], dict(dz=2 * way))
                far[-3 * way, part] = copy(kv.at[p, 0, part], kv.at[POS[-3 * way], 0, part], dict(dz=way))
                shared.append(share(p, part))
    for part, way in ((1, 1), (0, -1)):
        (behind, ahead)[part][part]()
        p = POS[-2 * way]
        far[-3 * way, part] = copy(kv.at[p, 0, part], kv.at[POS[-3 * way], 0, part], dict(dz=way))
        shared.append(share(p, part))
    done(beside)
    for d in (1, -1):
        shared.append(copy(kv.at[POS[d], 0], kv.at[POS[d], 1], dict(dc=1)))
    done(shared)

    def scores(h, ch):
        lo, hi = ((0, NEAR), (NEAR, ZS))[ch]
        n = (hi - lo) * 256
        for i in range(LANES // TOK):
            ry, rx = i // 2, (i % 2) * 2
            lanes = slice(h * LANES + i * TOK, h * LANES + i * TOK + TOK)
            here = slice(i * TOK, i * TOK + TOK)
            s = nt(kv[lo:hi, :, 0].reshape(n, HD), qb[h, ry, rx : rx + 2].reshape(TOK, HD)) * SCALE2
            t = nt(kv[lo:hi, :, 1].reshape(n, HD), gb[h, rx : rx + 2, ry].reshape(TOK, HD))
            sl[lo * 256 : hi * 256, lanes] = t
            s = s.reshape(n // 8, 8, TOK)
            peak = jnp.max(s, axis=0)
            w = jnp.exp2(s - peak[None])
            wt[lo * 256 : hi * 256, lanes] = w.reshape(n, TOK)
            pk[h, ch, :, here] = peak
            ms[h, ch, :, here] = jnp.sum(w, axis=0)
            mo[h, ch, :, here] = jnp.sum(w * t.reshape(n // 8, 8, TOK), axis=0)

    def local_statistics(h):
        top = jnp.maximum(pk[h, 0], pk[h, 1])
        row_top = jnp.max(top, axis=0, keepdims=True)
        near, far_off = jnp.exp2(pk[h, 0] - row_top), jnp.exp2(pk[h, 1] - row_top)
        mass = jnp.sum(ms[h, 0] * near + ms[h, 1] * far_off, axis=0, keepdims=True)
        moment = jnp.sum(mo[h, 0] * near + mo[h, 1] * far_off, axis=0, keepdims=True)
        log_mass = row_top + jnp.log2(mass)
        centre = moment / mass
        for i in range(LANES // TOK):
            st[h, 0, i : i + 1, :] = log_mass[:, i * TOK : i * TOK + TOK]
            st[h, 1, i : i + 1, :] = centre[:, i * TOK : i * TOK + TOK]

    def merge(parts):
        logs = [part[0] for part in parts]
        top = logs[0]
        for log in logs[1:]:
            top = jnp.maximum(top, log)
        weights = [jnp.exp2(log - top) for log in logs]
        mass = weights[0]
        moment = weights[0] * parts[0][1]
        for weight, part in zip(weights[1:], parts[1:]):
            mass = mass + weight
            moment = moment + weight * part[1]
        return top + jnp.log2(mass), moment / mass

    def along_x(h):
        return [copy(st.at[h], stx.at[h, d - 1], dict(dx=d)) for d in (1, 3, 2)]

    def along_y(h, waits):
        done(waits)
        log_mass, centre = merge([st.at[h]] + [stx.at[h, d] for d in range(3)])
        mid[h, 0] = log_mass
        mid[h, 1] = centre
        return [copy(mid.at[h], sty.at[h, d - 1], dict(dy=d)) for d in (1, 3, 2)]

    def settle(h, waits):
        done(waits)
        log_mass, centre = merge([mid.at[h]] + [sty.at[h, d] for d in range(3)])
        for i in range(LANES // TOK):
            here = slice(i * TOK, i * TOK + TOK)
            cs[h, :, here] = centre[i : i + 1, :]
            for ch in range(2):
                fs[h, ch, :, here] = jnp.exp2(pk[h, ch, :, here] - log_mass[i : i + 1, :])

    done(q_second[0] + g_second[0])
    scores(0, 0)
    last_shared = []
    for d, part in ((4, 0), (4, 1), (-3, 0), (3, 1), (-3, 1), (3, 0)):
        far[d, part]()
        last_shared.append(share(POS[d], part))
    done(q_second[1] + g_second[1])
    scores(1, 0)
    done(last_shared)
    scores(0, 1)
    local_statistics(0)
    first_x = along_x(0)
    scores(1, 1)
    local_statistics(1)
    second_x = along_x(1)
    first_y = along_y(0, first_x)
    second_y = along_y(1, second_x)

    def gradients(h, lo, hi):
        def block(p, carry):
            ch = p // NEAR
            cols = pl.ds(pl.multiple_of(p * 256, 256), 256)
            kt = kv[p, :, 0].reshape(256, HD).T
            if h == 0:
                dk = jnp.zeros((256, HD), F32)
                dv = jnp.zeros((256, HD), F32)
            else:
                dk = dkf[p].reshape(256, HD)
                dv = dvf[p].reshape(256, HD)
            for ry in range(YS):
                here = slice(ry * 256, ry * 256 + 256)
                lanes = slice(h * LANES + ry * 256, h * LANES + ry * 256 + 256)
                w = wt[cols, lanes].reshape(32, 8, 256)
                probs = (w * fs[h, ch, :, here][None]).reshape(256, 256)
                ds = (probs * (sl[cols, lanes] - cs[h, :, here])).astype(BF16)
                dk = dk + nn(ds, qb[h, ry].reshape(256, HD))
                dv = dv + nn(probs.astype(BF16), gb[h, :, ry].reshape(256, HD))
                dqt[h, :, here] += nn(kt, ds)
            dkf[p] = dk.reshape(2, TOK, HD)
            dvf[p] = dv.reshape(2, TOK, HD)
            return carry

        lax.fori_loop(lo, hi, block, 0, unroll=UNROLL)

    def query_start(h):
        for i in range(LANES // TOK):
            rows = dqt[h, :, i * TOK : i * TOK + TOK].T.astype(BF16)
            for b in range(2):
                ry, rx = i // 2, (i % 2) * 2 + b
                qa[h, ry, rx] = rows[b * HALF : b * HALF + HALF // 2]
                qc[h, rx, ry] = rows[b * HALF + HALF // 2 : b * HALF + HALF]
        a = [copy(qa.at[h, (y + d) % YS], qa_in.at[h, d - 1], dict(dy=d)) for d in (1, 3, 2)]
        b = [copy(qc.at[h, (x + d) % XS], qc_in.at[h, d - 1], dict(dx=d)) for d in (1, 3, 2)]
        return a, b

    def four(mine, others):
        total = mine.astype(F32)
        for n in range(3):
            total = total + others[n].astype(F32)
        return total

    def query_second(h, waits):
        done(waits[0])
        qa_mid[h] = four(qa[h, y], qa_in[h]).astype(BF16)
        a = [copy(qa_mid.at[h, (x + d) % XS], qa_fin.at[h, d - 1], dict(dx=d)) for d in (1, 3, 2)]
        done(waits[1])
        qc_mid[h] = four(qc[h, x], qc_in[h]).astype(BF16)
        b = [copy(qc_mid.at[h, (y + d) % YS], qc_fin.at[h, d - 1], dict(dy=d)) for d in (1, 3, 2)]
        return a + b

    def query_sum(h, waits):
        done(waits)
        return [four(qa_mid[h, x], qa_fin[h]), four(qc_mid[h, y], qc_fin[h])]

    def pair(lo, hi):
        waits = []
        for part, total in enumerate((dkf, dvf)):
            pair_out[part, lo:hi] = total[lo:hi, 1].astype(BF16)
            waits.append(copy(pair_out.at[part, lo:hi], pair_in.at[part, lo:hi], dict(dc=1)))
        return waits

    def whole(part, p):
        return (dkf, dvf)[part][p, 0] + pair_in[part, p].astype(F32)

    settle(0, first_y)
    gradients(0, 0, ZS)
    dq_first = query_start(0)
    settle(1, second_y)
    gradients(1, NEAR, ZS)
    pair_far = pair(NEAR, ZS)
    gradients(1, 3, NEAR)
    pair_mid = pair(3, NEAR)
    step = {}
    for part, way in ((0, 1), (1, -1)):
        pair_far[part]()
        for d in (4, 3, -3):
            red_out[part, POS[d]] = whole(part, POS[d]).astype(BF16)
        step[2, part] = copy(red_out.at[part, POS[4]], red_in.at[2, part], dict(dz=2 * way))
        step[0, part] = copy(red_out.at[part, POS[3]], red_in.at[0, part], dict(dz=1))
        step[1, part] = copy(red_out.at[part, POS[-3]], red_in.at[1, part], dict(dz=-1))
    gradients(1, 0, 3)
    pair_near = pair(0, 3)
    dq_second = query_start(1)
    dq_first = query_second(0, dq_first)
    done(pair_mid)
    done(pair_near)
    for n, d in ((3, 1), (4, -1)):
        for part in range(2):
            red_out[part, POS[d]] = whole(part, POS[d]).astype(BF16)
            step[n, part] = copy(red_out.at[part, POS[d]], red_in.at[n, part], dict(dz=d))
    for part in range(2):
        step[2, part]()
        for n, d in ((0, 2), (1, -2)):
            step[n, part]()
            total = whole(part, POS[d]) + red_in[n, part].astype(F32)
            if n == part:
                total = total + red_in[2, part].astype(F32)
            relay_out[n, part] = total.astype(BF16)
            step[5 + n, part] = copy(relay_out.at[n, part], red_in.at[5 + n, part], dict(dz=d))
    dq_second = query_second(1, dq_second)
    sums = query_sum(0, dq_first) + query_sum(1, dq_second)
    dq_ref[0] = (turned(jnp.concatenate(sums, axis=0), fwd[...], 1) * SCALE).astype(BF16)
    for part, (out, factor) in enumerate(((dk_ref, SCALE), (dv_ref, 1.0))):
        total = whole(part, 0)
        for n in (3, 4, 5, 6):
            step[n, part]()
            total = total + red_in[n, part].astype(F32)
        out[0] = (turned(total, bwd[...], 1) * factor).astype(BF16)
    for src, sem in pending:
        pltpu.make_async_copy(src, src, sem).wait()
    assert taken[0] <= SEMS


def per_device(queries, keys, values, out_grad, poses, pose_index):
    block = jax.ShapeDtypeStruct((1, TOK, HD), BF16)
    vmem = pl.BlockSpec(memory_space=pltpu.VMEM)
    smem = pl.BlockSpec(memory_space=pltpu.SMEM)

    def buf(*shape, kind=BF16):
        return pltpu.VMEM(shape, kind)

    part = HALF // 2
    return pl.pallas_call(
        kernel,
        out_shape=(block, block, block),
        in_specs=[vmem] * 4 + [smem] * 2,
        out_specs=(vmem, vmem, vmem),
        scratch_shapes=[
            buf(2, YS, XS, HALF, HD), buf(2, XS, YS, HALF, HD), buf(ZS, 2, 2, TOK, HD),
            buf(COLS, ROWS, kind=F32), buf(COLS, ROWS, kind=F32),
            buf(2, 2, 8, LANES, kind=F32), buf(2, 2, 8, LANES, kind=F32), buf(2, 2, 8, LANES, kind=F32),
            buf(2, 2, 8, TOK, kind=F32), buf(2, 3, 2, 8, TOK, kind=F32),
            buf(2, 2, 8, TOK, kind=F32), buf(2, 3, 2, 8, TOK, kind=F32),
            buf(2, 2, 8, LANES, kind=F32), buf(2, 1, LANES, kind=F32),
            buf(ZS, 2, TOK, HD, kind=F32), buf(ZS, 2, TOK, HD, kind=F32), buf(2, HD, LANES, kind=F32),
            buf(2, ZS, TOK, HD), buf(2, ZS, TOK, HD),
            buf(2, ZS, TOK, HD), buf(2, 2, TOK, HD), buf(7, 2, TOK, HD),
            buf(2, YS, XS, part, HD), buf(2, 3, XS, part, HD), buf(2, XS, part, HD), buf(2, 3, part, HD),
            buf(2, XS, YS, part, HD), buf(2, 3, YS, part, HD), buf(2, YS, part, HD), buf(2, 3, part, HD),
            buf(HD, HD, kind=F32), buf(HD, HD, kind=F32),
            pltpu.SemaphoreType.DMA((SEMS,)), pltpu.SemaphoreType.DMA((SEMS,)),
        ],
        compiler_params=pltpu.CompilerParams(
            collective_id=0, has_side_effects=True, vmem_limit_bytes=58 * 2**20
        ),
    )(queries, keys, values, out_grad, jnp.transpose(poses, (1, 2, 0)), pose_index)


def solution(mesh):
    block = P("view", "tok", None)
    return jax.shard_map(
        per_device, mesh=mesh, in_specs=(block,) * 4 + (P(), P()), out_specs=(block,) * 3, check_vma=False
    )
```

time: 78.3 us -> 58.7 us (0.75)
  the two profiles are of different devices: /device:TPU:2 before, /device:TPU:1 now
where the time goes in v2:
time: 58.7 us; the launch traced here: 58.4 us
  Pallas kernels  54.9 us (94%)
  local copies, waits for them, and re-layouts  2.77 us (5%)
  between operations  0.65 us (1%)
    pallas_call x1, Pallas kernels, per_device(): pl.pallas_call(kernel, out_shape=(block, block, block), in_specs=[vmem] *...  54.9 us
    unnamed x7, local copies, waits for them, and re-layouts  2.77 us

profile of v2, /device:TPU:1, one launch (start us, length us, event | category | flops | bytes accessed | tf_op | source)
XLA Modules:
  0.0 58.4 jit_solution(2922242798163509668)
XLA Ops:
  0.6 54.9 %shard_map.85 = (bf16[1,128,128]{2,1,0:T(8,128)(2,1)}, bf16[1,128,128]{2,1,0:T(8,128)(2,1)}, bf16[1,128,128]{2,1,0:T(8,128)(2,1)}) custom-call(bf16[1,128,128]{2,1,0:T(8,128)(2,1)} %q_ref.1, bf16[1,128,128]{2,1,0:T(8,128)(2,1)} %k_ref.1, bf16[1,128,128]{2,1,0:T(8,128)(2,1)} %v_ref.1, bf16[1,128,128]{2,1,0:T(8,128)(2,1)} %g_ref.1, f32[4,4,16]{2,1,0:T(4,128)} %bitcast.1, ...), custom_call_target="tpu_custom_call" | custom-call | tf_op jit(solution)/shard_map/pallas_call | solution.py:369
  55.6 0.0 copy-start.1
  55.6 1.4 %copy.12 = bf16[1,128,128]{2,1,0:T(8,128)(2,1)} copy(bf16[1,128,128]{2,1,0:T(8,128)(2,1)} %get-tuple-element.6) | data formatting | bytes 65536
  57.0 0.0 copy-done.1
  57.0 0.0 copy-start
  57.0 0.6 %copy.13 = bf16[1,128,128]{2,1,0:T(8,128)(2,1)} copy(bf16[1,128,128]{2,1,0:T(8,128)(2,1)S(1)} %copy-done.1) | data formatting | bytes 65536
  57.6 0.2 copy-done
  57.7 0.6 %copy.14 = bf16[1,128,128]{2,1,0:T(8,128)(2,1)} copy(bf16[1,128,128]{2,1,0:T(8,128)(2,1)S(1)} %copy-done) | data formatting | bytes 65536
Async XLA Ops:
  55.6 1.4 %copy-start.1 = (bf16[1,128,128]{2,1,0:T(8,128)(2,1)S(1)}, bf16[1,128,128]{2,1,0:T(8,128)(2,1)}, u32[]{:S(2)}) copy-start(bf16[1,128,128]{2,1,0:T(8,128)(2,1)} %get-tuple-element.7) | copy-start | bytes 98308
  57.0 0.8 %copy-start = (bf16[1,128,128]{2,1,0:T(8,128)(2,1)S(1)}, bf16[1,128,128]{2,1,0:T(8,128)(2,1)}, u32[]{:S(2)}) copy-start(bf16[1,128,128]{2,1,0:T(8,128)(2,1)} %get-tuple-element.8) | copy-start | bytes 98308

commit v3 on v2

--- a/solution.py
+++ b/solution.py
@@ -17,12 +17,14 @@
 COLS = ZS * 2 * TOK
 SCALE = HD**-0.5
 SCALE2 = SCALE / math.log(2.0)
-SEMS = 128
+RECV_SEMS = 55
+SEND_SEMS = 4
+BUCKET = 2**20
 HALF = TOK // 2
 LANES = ROWS // 2
 DIST = (0, 1, -1, 2, -2, 3, -3, 4)
 POS = {d: p for p, d in enumerate(DIST)}
-UNROLL = 1
+UNROLL = True
 NEAR = 5
 
 
@@ -63,7 +65,7 @@
 
 
 def kernel(
-    q_ref, k_ref, v_ref, g_ref, poses, pose_index, dq_ref, dk_ref, dv_ref,
+    q_ref, k_ref, v_ref, g_ref, poses, pose_index, out_ref,
     qb, gb, kv, wt, sl, pk, ms, mo, st, stx, mid, sty, fs, cs, dkf, dvf, dqt,
     pair_out, pair_in, red_out, relay_out, red_in,
     qa, qa_in, qa_mid, qa_fin, qc, qc_in, qc_mid, qc_fin, fwd, bwd, send_sem, recv_sem,
@@ -75,24 +77,37 @@
     z = (tok // 2) % 8
     c = tok % 2
     taken = [0]
-    pending = []
+    sent = [0]
 
     def device(dx=0, dy=0, dz=0, dc=0):
         px, py, pz, pc = (x + dx) % XS, (y + dy) % YS, (z + dz + ZS) % ZS, (c + dc) % 2
         return (py * 2 + px % 2, ((px // 2) * ZS + pz) * 2 + pc)
 
-    def copy(src, dst, to, arrives=None):
+    def amount(ref):
+        return math.prod(ref.shape) * jnp.dtype(ref.dtype).itemsize
+
+    def settle_bytes(total, sem):
+        rows = total // (4 * HD)
+        span = wt.at[:rows, :HD]
+        pltpu.make_async_copy(span, span, sem).wait()
+
+    def copies(*sends):
         n = taken[0]
         taken[0] += 1
-        arrives = dst if arrives is None else arrives
-        pltpu.make_async_remote_copy(
-            src_ref=src, dst_ref=dst, send_sem=send_sem.at[n], recv_sem=recv_sem.at[n],
-            device_id=device(**to), device_id_type=MESH,
-        ).start()
-        pending.append((src, send_sem.at[n]))
-        return lambda: pltpu.make_async_copy(arrives, arrives, recv_sem.at[n]).wait()
-
-    def done(waits):
+        total = 0
+        for src, dst, to in sends:
+            size = amount(src)
+            total += size
+            if sent[-1] + size > BUCKET:
+                sent.append(0)
+            sent[-1] += size
+            pltpu.make_async_remote_copy(
+                src_ref=src, dst_ref=dst, send_sem=send_sem.at[len(sent) - 1], recv_sem=recv_sem.at[n],
+                device_id=device(**to), device_id_type=MESH,
+            ).start()
+        return lambda: settle_bytes(total, recv_sem.at[n])
+
+    def done(*waits):
         for wait in waits:
             wait()
 
@@ -115,57 +130,54 @@
     dqt[...] = jnp.zeros_like(dqt)
     pl.semaphore_wait(barrier, len(peers))
 
+    def onward(p, part, to_p, distance):
+        return (kv.at[p, 0, part], kv.at[to_p, 0, part], dict(dz=distance))
+
     ahead, behind = [None, None], [None, None]
-    ahead[0] = copy(kv.at[0, 0, 0], kv.at[POS[-2], 0, 0], dict(dz=2))
-    behind[1] = copy(kv.at[0, 0, 1], kv.at[POS[2], 0, 1], dict(dz=-2))
-    q_first, g_first, q_second, g_second = [], [], [], []
+    ahead[0] = copies(onward(0, 0, POS[-2], 2))
+    behind[1] = copies(onward(0, 1, POS[2], -2))
+    first, second = [], []
     for h in range(2):
-        q_first.append([
-            copy(qb.at[h, y, x], qb.at[h, y, x], dict(dx=d), qb.at[h, y, (x + XS - d) % XS]) for d in (1, 3, 2)
-        ])
-        g_first.append([
-            copy(gb.at[h, x, y], gb.at[h, x, y], dict(dy=d), gb.at[h, x, (y + YS - d) % YS]) for d in (1, 3, 2)
+        first.append([
+            copies(*[(qb.at[h, y, x], qb.at[h, y, x], dict(dx=d)) for d in (1, 3, 2)]),
+            copies(*[(gb.at[h, x, y], gb.at[h, x, y], dict(dy=d)) for d in (1, 3, 2)]),
         ])
         if h == 0:
-            ahead[1] = copy(kv.at[0, 0, 1], kv.at[POS[-2], 0, 1], dict(dz=2))
-            behind[0] = copy(kv.at[0, 0, 0], kv.at[POS[2], 0, 0], dict(dz=-2))
-    shared = [copy(kv.at[0, 0], kv.at[0, 1], dict(dc=1))]
-    beside = [copy(kv.at[0, 0], kv.at[POS[-1], 0], dict(dz=1)), copy(kv.at[0, 0], kv.at[POS[1], 0], dict(dz=-1))]
-
-    def share(p, part):
-        return copy(kv.at[p, 0, part], kv.at[p, 1, part], dict(dc=1))
+            ahead[1] = copies(onward(0, 1, POS[-2], 2))
+            behind[0] = copies(onward(0, 0, POS[2], -2))
+    shared = [copies((kv.at[0, 0], kv.at[0, 1], dict(dc=1)))]
+    beside = copies((kv.at[0, 0], kv.at[POS[-1], 0], dict(dz=1)), (kv.at[0, 0], kv.at[POS[1], 0], dict(dz=-1)))
+
+    def share(*pieces):
+        return copies(*[(kv.at[p, 0, part], kv.at[p, 1, part], dict(dc=1)) for p, part in pieces])
 
     for h in range(2):
-        done(q_first[h])
-        q_second.append([
-            copy(qb.at[h, y], qb.at[h, y], dict(dy=d), qb.at[h, (y + YS - d) % YS]) for d in (1, 3, 2)
-        ])
-        done(g_first[h])
-        g_second.append([
-            copy(gb.at[h, x], gb.at[h, x], dict(dx=d), gb.at[h, (x + XS - d) % XS]) for d in (1, 3, 2)
-        ])
+        first[h][0]()
+        q_bundles = [(qb.at[h, y], qb.at[h, y], dict(dy=d)) for d in (1, 3, 2)]
         if h == 0:
             far = {}
             for part, way in ((0, 1), (1, -1)):
                 (ahead, behind)[part][part]()
                 p = POS[-2 * way]
-                far[4, part] = copy(kv.at[p, 0, part], kv.at[POS[4], 0, part], dict(dz=2 * way))
-                far[-3 * way, part] = copy(kv.at[p, 0, part], kv.at[POS[-3 * way], 0, part], dict(dz=way))
-                shared.append(share(p, part))
+                far[4, part] = copies(onward(p, part, POS[4], 2 * way))
+                far[-3 * way, part] = copies(onward(p, part, POS[-3 * way], way))
+                shared.append(share((p, part)))
+        first[h][1]()
+        g_bundles = [(gb.at[h, x], gb.at[h, x], dict(dx=d)) for d in (1, 3, 2)]
+        second.append(copies(*q_bundles, *g_bundles))
     for part, way in ((1, 1), (0, -1)):
         (behind, ahead)[part][part]()
         p = POS[-2 * way]
-        far[-3 * way, part] = copy(kv.at[p, 0, part], kv.at[POS[-3 * way], 0, part], dict(dz=way))
-        shared.append(share(p, part))
-    done(beside)
-    for d in (1, -1):
-        shared.append(copy(kv.at[POS[d], 0], kv.at[POS[d], 1], dict(dc=1)))
-    done(shared)
-
-    def scores(h, ch):
+        far[-3 * way, part] = copies(onward(p, part, POS[-3 * way], way))
+        shared.append(share((p, part)))
+    beside()
+    shared.append(share(*[(POS[d], part) for d in (1, -1) for part in range(2)]))
+    done(*shared)
+
+    def scores(h, ch, tiles=range(LANES // TOK)):
         lo, hi = ((0, NEAR), (NEAR, ZS))[ch]
         n = (hi - lo) * 256
-        for i in range(LANES // TOK):
+        for i in tiles:
             ry, rx = i // 2, (i % 2) * 2
             lanes = slice(h * LANES + i * TOK, h * LANES + i * TOK + TOK)
             here = slice(i * TOK, i * TOK + TOK)
@@ -206,17 +218,17 @@
         return top + jnp.log2(mass), moment / mass
 
     def along_x(h):
-        return [copy(st.at[h], stx.at[h, d - 1], dict(dx=d)) for d in (1, 3, 2)]
-
-    def along_y(h, waits):
-        done(waits)
+        return copies(*[(st.at[h], stx.at[h, d - 1], dict(dx=d)) for d in (1, 3, 2)])
+
+    def along_y(h, wait):
+        wait()
         log_mass, centre = merge([st.at[h]] + [stx.at[h, d] for d in range(3)])
         mid[h, 0] = log_mass
         mid[h, 1] = centre
-        return [copy(mid.at[h], sty.at[h, d - 1], dict(dy=d)) for d in (1, 3, 2)]
-
-    def settle(h, waits):
-        done(waits)
+        return copies(*[(mid.at[h], sty.at[h, d - 1], dict(dy=d)) for d in (1, 3, 2)])
+
+    def settle(h, wait):
+        wait()
         log_mass, centre = merge([mid.at[h]] + [sty.at[h, d] for d in range(3)])
         for i in range(LANES // TOK):
             here = slice(i * TOK, i * TOK + TOK)
@@ -224,15 +236,16 @@
             for ch in range(2):
                 fs[h, ch, :, here] = jnp.exp2(pk[h, ch, :, here] - log_mass[i : i + 1, :])
 
-    done(q_second[0] + g_second[0])
-    scores(0, 0)
+    second[0]()
+    scores(0, 0, range(0, 4))
     last_shared = []
     for d, part in ((4, 0), (4, 1), (-3, 0), (3, 1), (-3, 1), (3, 0)):
         far[d, part]()
-        last_shared.append(share(POS[d], part))
-    done(q_second[1] + g_second[1])
+        last_shared.append(share((POS[d], part)))
+    scores(0, 0, range(4, 8))
+    second[1]()
     scores(1, 0)
-    done(last_shared)
+    done(*last_shared)
     scores(0, 1)
     local_statistics(0)
     first_x = along_x(0)
@@ -275,8 +288,8 @@
                 ry, rx = i // 2, (i % 2) * 2 + b
                 qa[h, ry, rx] = rows[b * HALF : b * HALF + HALF // 2]
                 qc[h, rx, ry] = rows[b * HALF + HALF // 2 : b * HALF + HALF]
-        a = [copy(qa.at[h, (y + d) % YS], qa_in.at[h, d - 1], dict(dy=d)) for d in (1, 3, 2)]
-        b = [copy(qc.at[h, (x + d) % XS], qc_in.at[h, d - 1], dict(dx=d)) for d in (1, 3, 2)]
+        a = copies(*[(qa.at[h, (y + d) % YS], qa_in.at[h, d - 1], dict(dy=d)) for d in (1, 3, 2)])
+        b = copies(*[(qc.at[h, (x + d) % XS], qc_in.at[h, d - 1], dict(dx=d)) for d in (1, 3, 2)])
         return a, b
 
     def four(mine, others):
@@ -286,79 +299,84 @@
         return total
 
     def query_second(h, waits):
-        done(waits[0])
+        waits[0]()
         qa_mid[h] = four(qa[h, y], qa_in[h]).astype(BF16)
-        a = [copy(qa_mid.at[h, (x + d) % XS], qa_fin.at[h, d - 1], dict(dx=d)) for d in (1, 3, 2)]
-        done(waits[1])
+        a = copies(*[(qa_mid.at[h, (x + d) % XS], qa_fin.at[h, d - 1], dict(dx=d)) for d in (1, 3, 2)])
+        waits[1]()
         qc_mid[h] = four(qc[h, x], qc_in[h]).astype(BF16)
-        b = [copy(qc_mid.at[h, (y + d) % YS], qc_fin.at[h, d - 1], dict(dy=d)) for d in (1, 3, 2)]
-        return a + b
+        b = copies(*[(qc_mid.at[h, (y + d) % YS], qc_fin.at[h, d - 1], dict(dy=d)) for d in (1, 3, 2)])
+        return a, b
 
     def query_sum(h, waits):
-        done(waits)
+        done(*waits)
         return [four(qa_mid[h, x], qa_fin[h]), four(qc_mid[h, y], qc_fin[h])]
 
     def pair(lo, hi):
-        waits = []
+        sends = []
         for part, total in enumerate((dkf, dvf)):
             pair_out[part, lo:hi] = total[lo:hi, 1].astype(BF16)
-            waits.append(copy(pair_out.at[part, lo:hi], pair_in.at[part, lo:hi], dict(dc=1)))
-        return waits
+            sends.append((pair_out.at[part, lo:hi], pair_in.at[part, lo:hi], dict(dc=1)))
+        return copies(*sends)
 
     def whole(part, p):
         return (dkf, dvf)[part][p, 0] + pair_in[part, p].astype(F32)
 
     settle(0, first_y)
-    gradients(0, 0, ZS)
-    dq_first = query_start(0)
+    gradients(0, NEAR, ZS)
     settle(1, second_y)
     gradients(1, NEAR, ZS)
     pair_far = pair(NEAR, ZS)
-    gradients(1, 3, NEAR)
-    pair_mid = pair(3, NEAR)
+    gradients(0, 0, 3)
+    pair_far()
     step = {}
     for part, way in ((0, 1), (1, -1)):
-        pair_far[part]()
         for d in (4, 3, -3):
             red_out[part, POS[d]] = whole(part, POS[d]).astype(BF16)
-        step[2, part] = copy(red_out.at[part, POS[4]], red_in.at[2, part], dict(dz=2 * way))
-        step[0, part] = copy(red_out.at[part, POS[3]], red_in.at[0, part], dict(dz=1))
-        step[1, part] = copy(red_out.at[part, POS[-3]], red_in.at[1, part], dict(dz=-1))
+        step[2, part] = copies((red_out.at[part, POS[4]], red_in.at[2, part], dict(dz=2 * way)))
+        step[0, part] = copies((red_out.at[part, POS[3]], red_in.at[0, part], dict(dz=1)))
+        step[1, part] = copies((red_out.at[part, POS[-3]], red_in.at[1, part], dict(dz=-1)))
     gradients(1, 0, 3)
     pair_near = pair(0, 3)
-    dq_second = query_start(1)
-    dq_first = query_second(0, dq_first)
-    done(pair_mid)
-    done(pair_near)
+    gradients(0, 3, NEAR)
+    pair_near()
+    sends = []
     for n, d in ((3, 1), (4, -1)):
         for part in range(2):
             red_out[part, POS[d]] = whole(part, POS[d]).astype(BF16)
-            step[n, part] = copy(red_out.at[part, POS[d]], red_in.at[n, part], dict(dz=d))
-    for part in range(2):
-        step[2, part]()
-        for n, d in ((0, 2), (1, -2)):
-            step[n, part]()
-            total = whole(part, POS[d]) + red_in[n, part].astype(F32)
-            if n == part:
-                total = total + red_in[2, part].astype(F32)
-            relay_out[n, part] = total.astype(BF16)
-            step[5 + n, part] = copy(relay_out.at[n, part], red_in.at[5 + n, part], dict(dz=d))
+            sends.append((red_out.at[part, POS[d]], red_in.at[n, part], dict(dz=d)))
+    direct = copies(*sends)
+    dq_first = query_start(0)
+    gradients(1, 3, NEAR)
+    pair_mid = pair(3, NEAR)
+    dq_second = query_start(1)
+    dq_first = query_second(0, dq_first)
+    pair_mid()
+    relayed = []
+    for n, part in ((1, 0), (0, 0), (1, 1), (0, 1)):
+        d = (2, -2)[n]
+        step[n, part]()
+        total = whole(part, POS[d]) + red_in[n, part].astype(F32)
+        if n == part:
+            step[2, part]()
+            total = total + red_in[2, part].astype(F32)
+        relay_out[n, part] = total.astype(BF16)
+        relayed.append(copies((relay_out.at[n, part], red_in.at[5 + n, part], dict(dz=d))))
     dq_second = query_second(1, dq_second)
     sums = query_sum(0, dq_first) + query_sum(1, dq_second)
-    dq_ref[0] = (turned(jnp.concatenate(sums, axis=0), fwd[...], 1) * SCALE).astype(BF16)
-    for part, (out, factor) in enumerate(((dk_ref, SCALE), (dv_ref, 1.0))):
+    out_ref[0] = (turned(jnp.concatenate(sums, axis=0), fwd[...], 1) * SCALE).astype(BF16)
+    direct()
+    done(*relayed)
+    for part, factor in enumerate((SCALE, 1.0)):
         total = whole(part, 0)
         for n in (3, 4, 5, 6):
-            step[n, part]()
             total = total + red_in[n, part].astype(F32)
-        out[0] = (turned(total, bwd[...], 1) * factor).astype(BF16)
-    for src, sem in pending:
-        pltpu.make_async_copy(src, src, sem).wait()
-    assert taken[0] <= SEMS
+        out_ref[1 + part] = (turned(total, bwd[...], 1) * factor).astype(BF16)
+    for n, total in enumerate(sent):
+        settle_bytes(total, send_sem.at[n])
+    assert taken[0] <= RECV_SEMS and len(sent) <= SEND_SEMS
 
 
 def per_device(queries, keys, values, out_grad, poses, pose_index):
-    block = jax.ShapeDtypeStruct((1, TOK, HD), BF16)
     vmem = pl.BlockSpec(memory_space=pltpu.VMEM)
     smem = pl.BlockSpec(memory_space=pltpu.SMEM)
 
@@ -366,11 +384,11 @@
         return pltpu.VMEM(shape, kind)
 
     part = HALF // 2
-    return pl.pallas_call(
+    out = pl.pallas_call(
         kernel,
-        out_shape=(block, block, block),
+        out_shape=jax.ShapeDtypeStruct((3, TOK, HD), BF16),
         in_specs=[vmem] * 4 + [smem] * 2,
-        out_specs=(vmem, vmem, vmem),
+        out_specs=vmem,
         scratch_shapes=[
             buf(2, YS, XS, HALF, HD), buf(2, XS, YS, HALF, HD), buf(ZS, 2, 2, TOK, HD),
             buf(COLS, ROWS, kind=F32), buf(COLS, ROWS, kind=F32),
@@ -384,12 +402,13 @@
             buf(2, YS, XS, part, HD), buf(2, 3, XS, part, HD), buf(2, XS, part, HD), buf(2, 3, part, HD),
             buf(2, XS, YS, part, HD), buf(2, 3, YS, part, HD), buf(2, YS, part, HD), buf(2, 3, part, HD),
             buf(HD, HD, kind=F32), buf(HD, HD, kind=F32),
-            pltpu.SemaphoreType.DMA((SEMS,)), pltpu.SemaphoreType.DMA((SEMS,)),
+            pltpu.SemaphoreType.DMA((SEND_SEMS,)), pltpu.SemaphoreType.DMA((RECV_SEMS,)),
         ],
         compiler_params=pltpu.CompilerParams(
             collective_id=0, has_side_effects=True, vmem_limit_bytes=58 * 2**20
         ),
     )(queries, keys, values, out_grad, jnp.transpose(poses, (1, 2, 0)), pose_index)
+    return out[0:1], out[1:2], out[2:3]
 
 
 def solution(mesh):

time: 58.7 us -> 52.6 us (0.90)
  Pallas kernels: 54.9 us -> 50.2 us
  local copies, waits for them, and re-layouts: 2.77 us -> 1.43 us
    pallas_call x1, Pallas kernels: 54.9 us -> 50.2 us  [per_device(): pl.pallas_call(kernel, out_shape=jax.ShapeDtypeStruct((3, TOK, HD), BF16)...]
    unnamed x7 -> x0, local copies, waits for them, and re-layouts: 2.77 us -> none
    slice x0 -> x1, local copies, waits for them, and re-layouts: none -> 1.43 us  [per_device(): return (out[0:1], out[1:2], out[2:3])]
where the time goes in v3:
time: 52.6 us; the launch traced here: 52.3 us
  Pallas kernels  50.2 us (95%)
  local copies, waits for them, and re-layouts  1.43 us (3%)
  between operations  0.64 us (1%)
    pallas_call x1, Pallas kernels, per_device(): pl.pallas_call(kernel, out_shape=jax.ShapeDtypeStruct((3, TOK, HD), BF16)...  50.2 us
    slice x1, local copies, waits for them, and re-layouts, per_device(): return (out[0:1], out[1:2], out[2:3])  1.43 us

profile of v3, /device:TPU:1, one launch (start us, length us, event | category | flops | bytes accessed | tf_op | source)
XLA Modules:
  0.0 52.3 jit_solution(6163575741071966008)
XLA Ops:
  0.6 50.2 %shard_map.85 = bf16[3,128,128]{2,1,0:T(8,128)(2,1)} custom-call(bf16[1,128,128]{2,1,0:T(8,128)(2,1)} %q_ref.1, bf16[1,128,128]{2,1,0:T(8,128)(2,1)} %k_ref.1, bf16[1,128,128]{2,1,0:T(8,128)(2,1)} %v_ref.1, bf16[1,128,128]{2,1,0:T(8,128)(2,1)} %g_ref.1, f32[4,4,16]{2,1,0:T(4,128)} %bitcast.1, s32[8]{0:T(128)} %pose_index.1), custom_call_target="tpu_custom_call" | custom-call | tf_op jit(solution)/shard_map/pallas_call | solution.py:387
  50.9 1.4 %fusion = (bf16[1,128,128]{2,1,0:T(8,128)(2,1)}, bf16[1,128,128]{2,1,0:T(8,128)(2,1)}, bf16[1,128,128]{2,1,0:T(8,128)(2,1)}) fusion(bf16[3,128,128]{2,1,0:T(8,128)(2,1)} %shard_map.85), kind=kLoop, calls=%fused_computation | loop fusion | bytes 196608 | tf_op jit(solution)/shard_map/slice | solution.py:411

commit v4 on v3

v4 whole, which is shorter than its diff:
```python
import math

import jax
import jax.numpy as jnp
from jax import lax
from jax.experimental import pallas as pl
from jax.experimental.pallas import tpu as pltpu
from jax.sharding import PartitionSpec as P

F32 = jnp.float32
BF16 = jnp.bfloat16
MESH = pl.DeviceIdType.MESH
HD = 128
TOK = 128
XS, YS, ZS = 4, 4, 8
ROWS = XS * YS * TOK
COLS = ZS * 2 * TOK
SCALE = HD**-0.5
SCALE2 = SCALE / math.log(2.0)
RECV_SEMS = 46
SEND_SEMS = 4
BUCKET = 2**20
HALF = TOK // 2
LANES = ROWS // 2
TILES = ROWS // TOK
DIST = (0, 1, -1, 2, -2, 3, -3, 4)
POS = {d: p for p, d in enumerate(DIST)}
NEAR = 5


def nt(a, b):
    return lax.dot_general(a, b, (((1,), (1,)), ((), ())), preferred_element_type=F32)


def nn(a, b):
    return lax.dot_general(a, b, (((1,), (0,)), ((), ())), preferred_element_type=F32)


def turned(a, b, b_dim):
    return lax.dot_general(
        a, b, (((1,), (b_dim,)), ((), ())),
        precision=lax.Precision.HIGHEST, preferred_element_type=F32,
    )


def tables(poses, pose_index, view):
    row = pose_index[view]
    mat = [[poses[i, j, row] for j in range(4)] for i in range(4)]
    back = [[mat[i][j] for j in range(3)] + [mat[3][i]] for i in range(3)]
    back.append(
        [-(mat[0][j] * mat[0][3] + mat[1][j] * mat[1][3] + mat[2][j] * mat[2][3]) for j in range(3)]
        + [mat[3][3]]
    )
    i = lax.broadcasted_iota(jnp.int32, (HD, HD), 0)
    j = lax.broadcasted_iota(jnp.int32, (HD, HD), 1)
    place = jnp.where(i // 4 == j // 4, (i % 4) * 4 + j % 4, 16)
    forward = jnp.zeros((HD, HD), F32)
    backward = jnp.zeros((HD, HD), F32)
    for a in range(4):
        for b in range(4):
            here = place == 4 * a + b
            forward = jnp.where(here, mat[a][b], forward)
            backward = jnp.where(here, back[a][b], backward)
    return forward, backward


def kernel(
    q_ref, k_ref, v_ref, g_ref, poses, pose_index, out_ref,
    qb, gb, kv, wt, sl, pk, ms, mo, st, stx, mid, sty, share_x, share_y, fs, cs, dst, dkf, dvf, dqt,
    pair_out, pair_in, red_out, relay_out, red_in,
    qa, qa_in, qa_mid, qa_fin, qc, qc_in, qc_mid, qc_fin, fwd, bwd, send_sem, recv_sem,
):
    view = lax.axis_index("view")
    tok = lax.axis_index("tok")
    y = view // 2
    x = (tok // 16) * 2 + view % 2
    z = (tok // 2) % 8
    c = tok % 2
    taken = [0]
    sent = [0]
    ring = (1, 3, 2)

    def device(dx=0, dy=0, dz=0, dc=0):
        px, py, pz, pc = (x + dx) % XS, (y + dy) % YS, (z + dz + ZS) % ZS, (c + dc) % 2
        return (py * 2 + px % 2, ((px // 2) * ZS + pz) * 2 + pc)

    def amount(ref):
        return math.prod(ref.shape) * jnp.dtype(ref.dtype).itemsize

    def settle_bytes(total, sem):
        rows = total // (4 * HD)
        span = wt.at[:rows, :HD]
        pltpu.make_async_copy(span, span, sem).wait()

    class Group:
        def __init__(self, *sends):
            self.n = taken[0]
            self.total = 0
            taken[0] += 1
            self.add(*sends)

        def add(self, *sends):
            for src, dst, to in sends:
                size = amount(src)
                self.total += size
                if sent[-1] + size > BUCKET:
                    sent.append(0)
                sent[-1] += size
                pltpu.make_async_remote_copy(
                    src_ref=src, dst_ref=dst, send_sem=send_sem.at[len(sent) - 1], recv_sem=recv_sem.at[self.n],
                    device_id=device(**to), device_id_type=MESH,
                ).start()

        def wait(self):
            settle_bytes(self.total, recv_sem.at[self.n])

    barrier = pltpu.get_barrier_semaphore()
    peers = [dict(dx=d) for d in ring] + [dict(dy=d) for d in ring]
    peers += [dict(dz=d) for d in (1, -1, 2, -2)] + [dict(dc=1)]
    for peer in peers:
        pl.semaphore_signal(barrier, inc=1, device_id=device(**peer), device_id_type=MESH)

    forward, backward = tables(poses, pose_index, view)
    fwd[...] = forward
    bwd[...] = backward
    for ref, buf in ((q_ref, qb), (g_ref, gb)):
        own = turned(ref[0].astype(F32), forward, 0).astype(BF16)
        buf[0, y, x] = own[:HALF]
        buf[1, x, y] = own[HALF:]
    kv[0, 0, 0] = turned(k_ref[0].astype(F32), backward, 0).astype(BF16)
    kv[0, 0, 1] = turned(v_ref[0].astype(F32), backward, 0).astype(BF16)
    dqt[...] = jnp.zeros_like(dqt)
    pl.semaphore_wait(barrier, len(peers))

    def rows_first(buf):
        return (
            Group(*[(buf.at[0, y, x], buf.at[0, y, x], dict(dx=d)) for d in ring]),
            Group(*[(buf.at[1, x, y], buf.at[1, x, y], dict(dy=d)) for d in ring]),
        )

    def rows_second(buf, first):
        first[0].wait()
        group = Group(*[(buf.at[0, y], buf.at[0, y], dict(dy=d)) for d in ring])
        first[1].wait()
        group.add(*[(buf.at[1, x], buf.at[1, x], dict(dx=d)) for d in ring])
        return group

    def onward(part, p, to_p, distance, span=slice(None)):
        return (kv.at[p, 0, part, span], kv.at[to_p, 0, part, span], dict(dz=distance))

    def across(part, *places):
        return [(kv.at[p, 0, part], kv.at[p, 1, part], dict(dc=1)) for p in places]

    def columns_first(part):
        ahead = Group(onward(part, 0, POS[-2], 2))
        behind = Group(onward(part, 0, POS[2], -2))
        beside = Group(onward(part, 0, POS[-1], 1), onward(part, 0, POS[1], -1))
        return ahead, behind, beside

    def columns_second(part, first, near):
        far = None
        for way, span in ((1, slice(0, HALF)), (-1, slice(HALF, TOK))):
            first[0 if way == 1 else 1].wait()
            p = POS[-2 * way]
            sends = (onward(part, p, POS[4], 2 * way, span), onward(part, p, POS[-3 * way], way))
            if far is None:
                far = Group(*sends)
            else:
                far.add(*sends)
            near.add(*across(part, p))
        first[2].wait()
        near.add(*across(part, POS[1], POS[-1]))
        return far

    keys_first = columns_first(0)
    q_first = rows_first(qb)
    keys_near = Group(*across(0, 0))
    values_first = columns_first(1)
    g_first = rows_first(gb)
    values_near = Group(*across(1, 0))
    q_second = rows_second(qb, q_first)
    keys_far = columns_second(0, keys_first, keys_near)
    g_second = rows_second(gb, g_first)
    values_far = columns_second(1, values_first, values_near)

    def tile(buf, i):
        h, i = i // 8, i % 8
        ry, rx = i // 2, (i % 2) * 2
        part = buf[0, ry, rx : rx + 2] if h == 0 else buf[1, rx : rx + 2, ry]
        return part.reshape(TOK, HD)

    def wide(buf, i):
        return (buf[0, i] if i < YS else buf[1, :, i - YS]).reshape(2 * TOK, HD)

    def bounds(ch):
        lo, hi = ((0, NEAR), (NEAR, ZS))[ch]
        return lo, hi, slice(lo * 256, hi * 256), (hi - lo) * 256

    def scores(ch, tiles=range(TILES)):
        lo, hi, cols, n = bounds(ch)
        for i in tiles:
            lanes = slice(i * TOK, i * TOK + TOK)
            s = nt(kv[lo:hi, :, 0].reshape(n, HD), tile(qb, i)) * SCALE2
            s = s.reshape(hi - lo, 32, 8, TOK)
            peak = jnp.max(s, axis=1)
            w = jnp.exp2(s - peak[:, None])
            wt[cols, lanes] = w.reshape(n, TOK)
            pk[lo:hi, :, lanes] = peak
            ms[lo:hi, :, lanes] = jnp.sum(w, axis=1)

    def slopes(ch, tiles=range(TILES)):
        lo, hi, cols, n = bounds(ch)
        for i in tiles:
            lanes = slice(i * TOK, i * TOK + TOK)
            t = nt(kv[lo:hi, :, 1].reshape(n, HD), tile(gb, i))
            sl[cols, lanes] = t
            w = wt[cols, lanes].reshape(hi - lo, 32, 8, TOK)
            mo[lo:hi, :, lanes] = jnp.sum(w * t.reshape(hi - lo, 32, 8, TOK), axis=1)

    def local_mass():
        for i in range(TILES):
            lanes = slice(i * TOK, i * TOK + TOK)
            peak = pk[:, :, lanes]
            top = jnp.max(jnp.max(peak, axis=0), axis=0, keepdims=True)
            mass = jnp.sum(jnp.sum(ms[:, :, lanes] * jnp.exp2(peak - top[None]), axis=0), axis=0, keepdims=True)
            log_mass = top + jnp.log2(mass)
            cs[:, lanes] = log_mass
            st[0, i : i + 1, :] = log_mass

    def local_centre():
        for i in range(TILES):
            lanes = slice(i * TOK, i * TOK + TOK)
            factor = jnp.exp2(pk[:, :, lanes] - cs[:, lanes][None])
            st[1, i : i + 1, :] = jnp.sum(jnp.sum(mo[:, :, lanes] * factor, axis=0), axis=0, keepdims=True)

    def spread(src, landing, n, axis):
        return Group(*[(src.at[n], landing.at[n, d - 1], {axis: d}) for d in ring])

    def merge_mass(mine, landing, shares):
        logs = [mine[0]] + [landing[0, n] for n in range(3)]
        top = jnp.maximum(jnp.maximum(logs[0], logs[1]), jnp.maximum(logs[2], logs[3]))
        weights = [jnp.exp2(log - top) for log in logs]
        mass = weights[0] + weights[1] + weights[2] + weights[3]
        for n in range(4):
            shares[n] = weights[n] / mass
        return top + jnp.log2(mass)

    def merge_centre(mine, landing, shares):
        total = mine[1] * shares[0]
        for n in range(3):
            total = total + landing[1, n] * shares[n + 1]
        return total

    q_second.wait()
    keys_near.wait()
    scores(0, range(0, 8))
    keys_far.wait()
    keys_last = Group(*across(0, POS[4], POS[3], POS[-3]))
    scores(0, range(8, TILES))
    keys_last.wait()
    scores(1)
    local_mass()
    mass_x = spread(st, stx, 0, "dx")
    values_far.wait()
    values_last = Group(*across(1, POS[4], POS[3], POS[-3]))
    g_second.wait()
    values_near.wait()
    slopes(0)
    mass_x.wait()
    mid[0] = merge_mass(st, stx, share_x)
    mass_y = spread(mid, sty, 0, "dy")
    values_last.wait()
    slopes(1)
    local_centre()
    centre_x = spread(st, stx, 1, "dx")
    mass_y.wait()
    log_mass = merge_mass(mid, sty, share_y)
    for i in range(TILES):
        lanes = slice(i * TOK, i * TOK + TOK)
        fs[:, :, lanes] = jnp.exp2(pk[:, :, lanes] - log_mass[i : i + 1, :][None])

    def probabilities(p, cols, here):
        w = wt[cols, here].reshape(32, 8, 256)
        return (w * fs[p, :, here][None]).reshape(256, 256)

    def value_gradients(lo, hi):
        for p in range(lo, hi):
            dv = jnp.zeros((256, HD), F32)
            for i in range(ROWS // 256):
                here = slice(i * 256, i * 256 + 256)
                probs = probabilities(p, slice(p * 256, p * 256 + 256), here)
                dv = dv + nn(probs.astype(BF16), wide(gb, i))
            dvf[p] = dv.reshape(2, TOK, HD)

    def slope_gradients(p, kt, i):
        cols = slice(p * 256, p * 256 + 256)
        here = slice(i * 256, i * 256 + 256)
        ds = (probabilities(p, cols, here) * (sl[cols, here] - cs[:, here])).astype(BF16)
        dqt[:, here] += nn(kt, ds)
        return ds

    def key_gradients(lo, hi):
        for p in range(lo, hi):
            kt = kv[p, :, 0].reshape(256, HD).T
            dk = jnp.zeros((256, HD), F32)
            for i in range(ROWS // 256):
                dk = dk + nn(slope_gradients(p, kt, i), wide(qb, i))
            dkf[p] = dk.reshape(2, TOK, HD)

    def query_part(lo, hi, tiles):
        for p in range(lo, hi):
            kt = kv[p, :, 0].reshape(256, HD).T
            for i in tiles:
                dst[p * 256 : p * 256 + 256, i * 256 : i * 256 + 256] = slope_gradients(p, kt, i)

    def key_part(lo, hi):
        for p in range(lo, hi):
            dk = jnp.zeros((256, HD), F32)
            for i in range(ROWS // 256):
                dk = dk + nn(dst[p * 256 : p * 256 + 256, i * 256 : i * 256 + 256], wide(qb, i))
            dkf[p] = dk.reshape(2, TOK, HD)

    totals = (dkf, dvf)

    def pair(part, lo, hi):
        pair_out[part, lo:hi] = totals[part][lo:hi, 1].astype(BF16)
        return Group((pair_out.at[part, lo:hi], pair_in.at[part, lo:hi], dict(dc=1)))

    def whole(part, p):
        return totals[part][p, 0] + pair_in[part, p].astype(F32)

    def outward(part):
        for d in (4, 3, -3):
            red_out[part, POS[d]] = whole(part, POS[d]).astype(BF16)
        waits = []
        for n, way, span in ((0, 1, slice(0, HALF)), (1, -1, slice(HALF, TOK))):
            waits.append(Group(
                (red_out.at[part, POS[4], span], red_in.at[2, part, span], dict(dz=2 * way)),
                (red_out.at[part, POS[3 * way]], red_in.at[n, part], dict(dz=way)),
            ))
        return waits

    def direct(part):
        for d in (1, -1):
            red_out[part, POS[d]] = whole(part, POS[d]).astype(BF16)
        return Group(*[
            (red_out.at[part, POS[d]], red_in.at[n, part], dict(dz=d)) for n, d in ((3, 1), (4, -1))
        ])

    def relay(part, waits, group):
        for n, d, span in ((0, 2, slice(0, HALF)), (1, -2, slice(HALF, TOK))):
            waits[n].wait()
            rest = slice(HALF, TOK) if n == 0 else slice(0, HALF)
            total = whole(part, POS[d]) + red_in[n, part].astype(F32)
            relay_out[n, part, span] = (total[span] + red_in[2, part, span].astype(F32)).astype(BF16)
            relay_out[n, part, rest] = total[rest].astype(BF16)
            group.add((relay_out.at[n, part], red_in.at[5 + n, part], dict(dz=d)))

    def owned(part):
        total = whole(part, 0)
        for n in (3, 4, 5, 6):
            total = total + red_in[n, part].astype(F32)
        return total

    def query_start(h):
        for j in range(TILES // 2):
            i = h * (TILES // 2) + j
            rows = dqt[:, i * TOK : i * TOK + TOK].T.astype(BF16)
            for b in range(2):
                ry, rx = j // 2, (j % 2) * 2 + b
                qa[h, ry, rx] = rows[b * HALF : b * HALF + HALF // 2]
                qc[h, rx, ry] = rows[b * HALF + HALF // 2 : b * HALF + HALF]
        return (
            Group(*[(qa.at[h, (y + d) % YS], qa_in.at[h, d - 1], dict(dy=d)) for d in ring]),
            Group(*[(qc.at[h, (x + d) % XS], qc_in.at[h, d - 1], dict(dx=d)) for d in ring]),
        )

    def four(mine, others):
        total = mine.astype(F32)
        for n in range(3):
            total = total + others[n].astype(F32)
        return total

    def query_second(h, waits):
        waits[0].wait()
        qa_mid[h] = four(qa[h, y], qa_in[h]).astype(BF16)
        group = Group(*[(qa_mid.at[h, (x + d) % XS], qa_fin.at[h, d - 1], dict(dx=d)) for d in ring])
        waits[1].wait()
        qc_mid[h] = four(qc[h, x], qc_in[h]).astype(BF16)
        group.add(*[(qc_mid.at[h, (y + d) % YS], qc_fin.at[h, d - 1], dict(dy=d)) for d in ring])
        return group

    def query_sum(h):
        return [four(qa_mid[h, x], qa_fin[h]), four(qc_mid[h, y], qc_fin[h])]

    value_gradients(NEAR, ZS)
    pair_far = pair(1, NEAR, ZS)
    centre_x.wait()
    mid[1] = merge_centre(st, stx, share_x)
    centre_y = spread(mid, sty, 1, "dy")
    value_gradients(0, 3)
    pair_near = pair(1, 0, 3)
    pair_far.wait()
    values_out = outward(1)
    value_gradients(3, NEAR)
    pair_mid = pair(1, 3, NEAR)
    pair_near.wait()
    values_in = direct(1)
    centre_y.wait()
    centre = merge_centre(mid, sty, share_y)
    for i in range(TILES):
        cs[:, i * TOK : i * TOK + TOK] = centre[i : i + 1, :]
    key_gradients(NEAR, ZS)
    pair_far = pair(0, NEAR, ZS)
    query_part(0, NEAR, range(0, YS))
    queries_out = [query_start(0)]
    pair_far.wait()
    keys_out = outward(0)
    query_part(0, NEAR, range(YS, 2 * YS))
    queries_out.append(query_start(1))
    pair_mid.wait()
    relay(1, values_out, values_in)
    key_part(0, 3)
    pair_near = pair(0, 0, 3)
    key_part(3, NEAR)
    pair_mid = pair(0, 3, NEAR)
    pair_near.wait()
    keys_in = direct(0)
    pair_mid.wait()
    queries_in = [query_second(0, queries_out[0])]
    relay(0, keys_out, keys_in)
    queries_in.append(query_second(1, queries_out[1]))
    values_in.wait()
    out_ref[2] = turned(owned(1), bwd[...], 1).astype(BF16)
    queries_in[0].wait()
    queries_in[1].wait()
    dq = jnp.concatenate(query_sum(0) + query_sum(1), axis=0)
    out_ref[0] = (turned(dq, fwd[...], 1) * SCALE).astype(BF16)
    keys_in.wait()
    out_ref[1] = (turned(owned(0), bwd[...], 1) * SCALE).astype(BF16)
    for n, total in enumerate(sent):
        settle_bytes(total, send_sem.at[n])
    assert taken[0] <= RECV_SEMS and len(sent) <= SEND_SEMS


def per_device(queries, keys, values, out_grad, poses, pose_index):
    vmem = pl.BlockSpec(memory_space=pltpu.VMEM)
    smem = pl.BlockSpec(memory_space=pltpu.SMEM)

    def buf(*shape, kind=BF16):
        return pltpu.VMEM(shape, kind)

    part = HALF // 2
    out = pl.pallas_call(
        kernel,
        out_shape=jax.ShapeDtypeStruct((3, TOK, HD), BF16),
        in_specs=[vmem] * 4 + [smem] * 2,
        out_specs=vmem,
        scratch_shapes=[
            buf(2, YS, XS, HALF, HD), buf(2, XS, YS, HALF, HD), buf(ZS, 2, 2, TOK, HD),
            buf(COLS, ROWS, kind=F32), buf(COLS, ROWS, kind=F32),
            *[buf(ZS, 8, ROWS, kind=F32)] * 3,
            buf(2, TILES, TOK, kind=F32), buf(2, 3, TILES, TOK, kind=F32),
            buf(2, TILES, TOK, kind=F32), buf(2, 3, TILES, TOK, kind=F32),
            buf(4, TILES, TOK, kind=F32), buf(4, TILES, TOK, kind=F32),
            buf(ZS, 8, ROWS, kind=F32), buf(1, ROWS, kind=F32), buf(NEAR * 256, ROWS),
            buf(ZS, 2, TOK, HD, kind=F32), buf(ZS, 2, TOK, HD, kind=F32), buf(HD, ROWS, kind=F32),
            buf(2, ZS, TOK, HD), buf(2, ZS, TOK, HD),
            buf(2, ZS, TOK, HD), buf(2, 2, TOK, HD), buf(7, 2, TOK, HD),
            buf(2, YS, XS, part, HD), buf(2, 3, XS, part, HD), buf(2, XS, part, HD), buf(2, 3, part, HD),
            buf(2, XS, YS, part, HD), buf(2, 3, YS, part, HD), buf(2, YS, part, HD), buf(2, 3, part, HD),
            buf(HD, HD, kind=F32), buf(HD, HD, kind=F32),
            pltpu.SemaphoreType.DMA((SEND_SEMS,)), pltpu.SemaphoreType.DMA((RECV_SEMS,)),
        ],
        compiler_params=pltpu.CompilerParams(
            collective_id=0, has_side_effects=True, vmem_limit_bytes=58 * 2**20
        ),
    )(queries, keys, values, out_grad, jnp.transpose(poses, (1, 2, 0)), pose_index)
    return out[0:1], out[1:2], out[2:3]


def solution(mesh):
    block = P("view", "tok", None)
    return jax.shard_map(
        per_device, mesh=mesh, in_specs=(block,) * 4 + (P(), P()), out_specs=(block,) * 3, check_vma=False
    )
```

time: 52.6 us -> 51.2 us (0.973)
  Pallas kernels: 50.2 us -> 48.9 us
    pallas_call x1, Pallas kernels: 50.2 us -> 48.9 us  [per_device(): pl.pallas_call(kernel, out_shape=jax.ShapeDtypeStruct((3, TOK, HD), BF16)...]
where the time goes in v4:
time: 51.2 us; the launch traced here: 51 us
  Pallas kernels  48.9 us (96%)
  local copies, waits for them, and re-layouts  1.43 us (3%)
  between operations  0.64 us (1%)
    pallas_call x1, Pallas kernels, per_device(): pl.pallas_call(kernel, out_shape=jax.ShapeDtypeStruct((3, TOK, HD), BF16)...  48.9 us
    slice x1, local copies, waits for them, and re-layouts, per_device(): return (out[0:1], out[1:2], out[2:3])  1.43 us

profile of v4, /device:TPU:1, one launch (start us, length us, event | category | flops | bytes accessed | tf_op | source)
XLA Modules:
  0.0 51.0 jit_solution(5826533609603159301)
XLA Ops:
  0.6 48.9 %shard_map.85 = bf16[3,128,128]{2,1,0:T(8,128)(2,1)} custom-call(bf16[1,128,128]{2,1,0:T(8,128)(2,1)} %q_ref.1, bf16[1,128,128]{2,1,0:T(8,128)(2,1)} %k_ref.1, bf16[1,128,128]{2,1,0:T(8,128)(2,1)} %v_ref.1, bf16[1,128,128]{2,1,0:T(8,128)(2,1)} %g_ref.1, f32[4,4,16]{2,1,0:T(4,128)} %bitcast.1, s32[8]{0:T(128)} %pose_index.1), custom_call_target="tpu_custom_call" | custom-call | tf_op jit(solution)/shard_map/pallas_call | solution.py:454
  49.5 1.4 %fusion = (bf16[1,128,128]{2,1,0:T(8,128)(2,1)}, bf16[1,128,128]{2,1,0:T(8,128)(2,1)}, bf16[1,128,128]{2,1,0:T(8,128)(2,1)}) fusion(bf16[3,128,128]{2,1,0:T(8,128)(2,1)} %shard_map.85), kind=kLoop, calls=%fused_computation | loop fusion | bytes 196608 | tf_op jit(solution)/shard_map/slice | solution.py:479

commit v5 on v4

--- a/solution.py
+++ b/solution.py
@@ -266,13 +266,16 @@
     g_second.wait()
     values_near.wait()
     slopes(0)
-    mass_x.wait()
-    mid[0] = merge_mass(st, stx, share_x)
-    mass_y = spread(mid, sty, 0, "dy")
     values_last.wait()
     slopes(1)
     local_centre()
     centre_x = spread(st, stx, 1, "dx")
+    mass_x.wait()
+    mid[0] = merge_mass(st, stx, share_x)
+    mass_y = spread(mid, sty, 0, "dy")
+    centre_x.wait()
+    mid[1] = merge_centre(st, stx, share_x)
+    centre_y = spread(mid, sty, 1, "dy")
     mass_y.wait()
     log_mass = merge_mass(mid, sty, share_y)
     for i in range(TILES):
@@ -340,12 +343,10 @@
             ))
         return waits
 
-    def direct(part):
+    def direct(part, group):
         for d in (1, -1):
             red_out[part, POS[d]] = whole(part, POS[d]).astype(BF16)
-        return Group(*[
-            (red_out.at[part, POS[d]], red_in.at[n, part], dict(dz=d)) for n, d in ((3, 1), (4, -1))
-        ])
+        group.add(*[(red_out.at[part, POS[d]], red_in.at[n, part], dict(dz=d)) for n, d in ((3, 1), (4, -1))])
 
     def relay(part, waits, group):
         for n, d, span in ((0, 2, slice(0, HALF)), (1, -2, slice(HALF, TOK))):
@@ -395,17 +396,10 @@
 
     value_gradients(NEAR, ZS)
     pair_far = pair(1, NEAR, ZS)
-    centre_x.wait()
-    mid[1] = merge_centre(st, stx, share_x)
-    centre_y = spread(mid, sty, 1, "dy")
-    value_gradients(0, 3)
-    pair_near = pair(1, 0, 3)
+    value_gradients(3, NEAR)
+    pair_mid = pair(1, 3, NEAR)
     pair_far.wait()
     values_out = outward(1)
-    value_gradients(3, NEAR)
-    pair_mid = pair(1, 3, NEAR)
-    pair_near.wait()
-    values_in = direct(1)
     centre_y.wait()
     centre = merge_centre(mid, sty, share_y)
     for i in range(TILES):
@@ -413,19 +407,25 @@
     key_gradients(NEAR, ZS)
     pair_far = pair(0, NEAR, ZS)
     query_part(0, NEAR, range(0, YS))
-    queries_out = [query_start(0)]
     pair_far.wait()
     keys_out = outward(0)
+    queries_out = [query_start(0)]
     query_part(0, NEAR, range(YS, 2 * YS))
     queries_out.append(query_start(1))
     pair_mid.wait()
+    value_gradients(0, 3)
+    pair_near = pair(1, 0, 3)
+    values_in = Group()
     relay(1, values_out, values_in)
     key_part(0, 3)
-    pair_near = pair(0, 0, 3)
+    keys_near = pair(0, 0, 3)
+    pair_near.wait()
+    direct(1, values_in)
     key_part(3, NEAR)
     pair_mid = pair(0, 3, NEAR)
-    pair_near.wait()
-    keys_in = direct(0)
+    keys_near.wait()
+    keys_in = Group()
+    direct(0, keys_in)
     pair_mid.wait()
     queries_in = [query_second(0, queries_out[0])]
     relay(0, keys_out, keys_in)

time: 51.2 us -> 50.3 us (0.982)
  Pallas kernels: 48.9 us -> 48 us
    pallas_call x1, Pallas kernels: 48.9 us -> 48 us  [per_device(): pl.pallas_call(kernel, out_shape=jax.ShapeDtypeStruct((3, TOK, HD), BF16)...]
where the time goes in v5:
time: 50.3 us; the launch traced here: 50 us
  Pallas kernels  48 us (95%)
  local copies, waits for them, and re-layouts  1.43 us (3%)
  between operations  0.64 us (1%)
    pallas_call x1, Pallas kernels, per_device(): pl.pallas_call(kernel, out_shape=jax.ShapeDtypeStruct((3, TOK, HD), BF16)...  48 us
    slice x1, local copies, waits for them, and re-layouts, per_device(): return (out[0:1], out[1:2], out[2:3])  1.43 us

profile of v5, /device:TPU:1, one launch (start us, length us, event | category | flops | bytes accessed | tf_op | source)
XLA Modules:
  0.0 50.0 jit_solution(2668164508884604560)
XLA Ops:
  0.6 48.0 %shard_map.85 = bf16[3,128,128]{2,1,0:T(8,128)(2,1)} custom-call(bf16[1,128,128]{2,1,0:T(8,128)(2,1)} %q_ref.1, bf16[1,128,128]{2,1,0:T(8,128)(2,1)} %k_ref.1, bf16[1,128,128]{2,1,0:T(8,128)(2,1)} %v_ref.1, bf16[1,128,128]{2,1,0:T(8,128)(2,1)} %g_ref.1, f32[4,4,16]{2,1,0:T(4,128)} %bitcast.1, s32[8]{0:T(128)} %pose_index.1), custom_call_target="tpu_custom_call" | custom-call | tf_op jit(solution)/shard_map/pallas_call | solution.py:454
  48.6 1.4 %fusion = (bf16[1,128,128]{2,1,0:T(8,128)(2,1)}, bf16[1,128,128]{2,1,0:T(8,128)(2,1)}, bf16[1,128,128]{2,1,0:T(8,128)(2,1)}) fusion(bf16[3,128,128]{2,1,0:T(8,128)(2,1)} %shard_map.85), kind=kLoop, calls=%fused_computation | loop fusion | bytes 196608 | tf_op jit(solution)/shard_map/slice | solution.py:479

commit v6 on v5

--- a/solution.py
+++ b/solution.py
@@ -421,13 +421,13 @@
     keys_near = pair(0, 0, 3)
     pair_near.wait()
     direct(1, values_in)
+    queries_in = [query_second(0, queries_out[0])]
     key_part(3, NEAR)
     pair_mid = pair(0, 3, NEAR)
     keys_near.wait()
     keys_in = Group()
     direct(0, keys_in)
     pair_mid.wait()
-    queries_in = [query_second(0, queries_out[0])]
     relay(0, keys_out, keys_in)
     queries_in.append(query_second(1, queries_out[1]))
     values_in.wait()

time: 50.3 us -> 51.7 us (1.028)
  Pallas kernels: 48 us -> 49.4 us
    pallas_call x1, Pallas kernels: 48 us -> 49.4 us  [per_device(): pl.pallas_call(kernel, out_shape=jax.ShapeDtypeStruct((3, TOK, HD), BF16)...]
where the time goes in v6:
time: 51.7 us; the launch traced here: 51.5 us
  Pallas kernels  49.4 us (96%)
  local copies, waits for them, and re-layouts  1.43 us (3%)
  between operations  0.64 us (1%)
    pallas_call x1, Pallas kernels, per_device(): pl.pallas_call(kernel, out_shape=jax.ShapeDtypeStruct((3, TOK, HD), BF16)...  49.4 us
    slice x1, local copies, waits for them, and re-layouts, per_device(): return (out[0:1], out[1:2], out[2:3])  1.43 us

profile of v6, /device:TPU:1, one launch (start us, length us, event | category | flops | bytes accessed | tf_op | source)
XLA Modules:
  0.0 51.5 jit_solution(6996663535656498357)
XLA Ops:
  0.6 49.4 %shard_map.85 = bf16[3,128,128]{2,1,0:T(8,128)(2,1)} custom-call(bf16[1,128,128]{2,1,0:T(8,128)(2,1)} %q_ref.1, bf16[1,128,128]{2,1,0:T(8,128)(2,1)} %k_ref.1, bf16[1,128,128]{2,1,0:T(8,128)(2,1)} %v_ref.1, bf16[1,128,128]{2,1,0:T(8,128)(2,1)} %g_ref.1, f32[4,4,16]{2,1,0:T(4,128)} %bitcast.1, s32[8]{0:T(128)} %pose_index.1), custom_call_target="tpu_custom_call" | custom-call | tf_op jit(solution)/shard_map/pallas_call | solution.py:454
  50.0 1.4 %fusion = (bf16[1,128,128]{2,1,0:T(8,128)(2,1)}, bf16[1,128,128]{2,1,0:T(8,128)(2,1)}, bf16[1,128,128]{2,1,0:T(8,128)(2,1)}) fusion(bf16[3,128,128]{2,1,0:T(8,128)(2,1)} %shard_map.85), kind=kLoop, calls=%fused_computation | loop fusion | bytes 196608 | tf_op jit(solution)/shard_map/slice | solution.py:479
